TPU v7x, 128 devices: a whole 4x4x4 slice. The times are simulated.
128 devices in a mesh: section: 8 (over z, core), dp: 2 (over x_lo), tensor: 8 (over x_hi, y).
Axes of the slice: x: 4 (x_hi: 2, x_lo: 2; x = x_hi * 2 + x_lo), y: 4, z: 4, core: 2. Of those that a mesh axis runs over, the one named last changes fastest.
Arguments:
- patches: bfloat16 [16, 1024, 3200], P(('section', 'dp'), 'tensor'), may hold values from -4 to 4
- norm_gain: float32 [3200], replicated, may hold values from 0.1 to 1.9
- w_qkv: bfloat16 [3200, 3, 3072], P(None, None, 'tensor')
- q_gain: float32 [3072], P('tensor')
- k_gain: float32 [3072], P('tensor')
- w_out: bfloat16 [3072, 3200], P('tensor'), may hold values from -0.109375 to 0.109375
- layer_scale: float32 [3200], replicated, may hold values from 0.5 to 1.5
- w_proj: bfloat16 [12800, 4096], P(None, 'tensor'), may hold values from -0.0546875 to 0.0546875
- text_embed: bfloat16 [16, 768, 4096], P(('section', 'dp'), None, 'tensor'), may hold values from -6 to 6
- tile_counts: int32 [16], replicated, may hold values from 0 to 2, as said below
- image_offsets: int32 [16], replicated, may hold values from 0 to 256
- tile_slots: int32 [16], replicated, may hold values from 0 to 15, as said below
Outputs:
- llm_input: bfloat16 [16, 768, 4096], P(('section', 'dp'), None, 'tensor')
Inputs may be any that keep to these rules, and one draw needn't show every extreme that they name: `tile_counts`: the counts sum to 16; the largest is exactly 2, and some sequence has no tile. `tile_slots`: a permutation of the packed positions.
All inputs are finite; a program needn't handle non-finite values.
Results may differ from a plain program's by a relative error of at most 0.012.
Values may be sent and summed in bfloat16 or wider, within the bound.
A program may use at most 128 MiB of HBM per device.

v0:
```python
import jax
import jax.numpy as jnp
from jax import lax
from jax.sharding import PartitionSpec as P

HEADS = 24
HD = 128
GRID = 32


def rms_scale(values, gain):
    mean_square = jnp.mean(values * values, axis=-1, keepdims=True)
    return values * lax.rsqrt(mean_square + 1e-06) * gain


def shards(
    patches,
    norm_gain,
    w_qkv,
    q_gain,
    k_gain,
    w_out,
    layer_scale,
    w_proj,
    text_embed,
    tile_counts,
    image_offsets,
    tile_slots,
):
    tiles_here, rows_here, width_d = patches.shape
    local_width = w_qkv.shape[2]
    local_heads = local_width // HD
    local_wl = w_proj.shape[1]
    patches_f = patches.astype(jnp.float32)
    normed = rms_scale(patches_f, norm_gain).astype(jnp.bfloat16)
    w_flat = w_qkv.reshape(width_d, 3 * local_width)
    shard_rows = lax.all_gather(normed, "tensor", axis=1, tiled=True)
    flat = jnp.dot(shard_rows.reshape(-1, width_d), w_flat, preferred_element_type=jnp.float32)
    stacked = flat.reshape(shard_rows.shape[0], shard_rows.shape[1], 3 * local_width)
    tile_len = stacked.shape[1]
    query_part = stacked[..., :local_width]
    key_part = stacked[..., local_width : 2 * local_width]
    value_part = stacked[..., 2 * local_width :]
    query_sq, key_sq = lax.psum(
        (jnp.sum(query_part * query_part, axis=-1), jnp.sum(key_part * key_part, axis=-1)), "tensor"
    )
    full_width = HEADS * HD
    queries = (query_part * lax.rsqrt(query_sq[..., None] / full_width + 1e-06) * q_gain).astype(
        jnp.bfloat16
    )
    key_rows = (key_part * lax.rsqrt(key_sq[..., None] / full_width + 1e-06) * k_gain).astype(
        jnp.bfloat16
    )
    value_rows = value_part.astype(jnp.bfloat16)
    queries = queries.reshape(tiles_here, tile_len, local_heads, HD)
    key_rows = key_rows.reshape(tiles_here, tile_len, local_heads, HD)
    value_rows = value_rows.reshape(tiles_here, tile_len, local_heads, HD)
    scores = jnp.einsum(
        "bqhd,bkhd->bhqk", queries, key_rows, preferred_element_type=jnp.float32
    ) * HD ** (-0.5)
    weights = jax.nn.softmax(scores, axis=-1).astype(jnp.bfloat16)
    mixed = jnp.einsum(
        "bhqk,bkhd->bqhd", weights, value_rows, preferred_element_type=jnp.float32
    ).astype(jnp.bfloat16)
    mixed_flat = mixed.reshape(tiles_here, tile_len, local_width)
    token_major = mixed_flat.transpose(1, 0, 2)
    flat = jnp.dot(token_major.reshape(-1, local_width), w_out, preferred_element_type=jnp.float32)
    branch = (
        lax.psum_scatter(
            flat.reshape(rows_here * lax.axis_size("tensor"), tiles_here, width_d).astype(
                jnp.bfloat16
            ),
            "tensor",
            scatter_dimension=0,
            tiled=True,
        )
        .astype(jnp.float32)
        .transpose(1, 0, 2)
    )
    encoded = (patches_f + layer_scale * branch).astype(jnp.bfloat16)
    half_grid = GRID // 2
    pair_rows = rows_here // (2 * GRID)
    merged = encoded.reshape(tiles_here, pair_rows, 2, half_grid, 2, width_d).transpose(
        0, 1, 3, 2, 4, 5
    )
    merged = merged.reshape(tiles_here, pair_rows * half_grid, 4 * width_d)
    shard_rows = lax.all_gather(merged, "tensor", axis=1, tiled=True)
    flat = jnp.dot(
        shard_rows.reshape(-1, shard_rows.shape[2]), w_proj, preferred_element_type=jnp.float32
    )
    projected = flat.reshape(shard_rows.shape[0], shard_rows.shape[1], local_wl).astype(
        jnp.bfloat16
    )
    out_len = projected.shape[1]
    group = lax.axis_index(("section", "dp"))
    tile_cap = 2 * tiles_here
    total_tiles = tile_slots.shape[0]
    first_tile = jnp.cumsum(tile_counts) - tile_counts
    my_first = first_tile[group]
    my_count = tile_counts[group]
    my_offset = image_offsets[group]
    slots = jnp.arange(tile_cap, dtype=jnp.int32)
    logical = jnp.minimum(my_first + slots, total_tiles - 1)
    wanted = jnp.take(tile_slots, logical, axis=0)
    live_slot = slots < my_count
    shard_tiles = lax.all_gather(projected, ("section", "dp"), axis=0, tiled=True)
    count_tiles = shard_tiles.shape[0]
    tile_ids = jnp.arange(count_tiles, dtype=jnp.int32)
    picks = (tile_ids[None, :] == wanted[:, None]) & live_slot[:, None]
    features = jnp.dot(
        picks.astype(jnp.bfloat16),
        shard_tiles.reshape(count_tiles, -1),
        preferred_element_type=jnp.float32,
    ).astype(jnp.bfloat16)
    block = features.reshape(tile_cap * out_len, local_wl)
    seq_len = text_embed.shape[1]
    placed = lax.dynamic_update_slice(
        jnp.zeros((seq_len, local_wl), jnp.bfloat16), block, (my_offset, jnp.int32(0))
    )
    positions = jnp.arange(seq_len, dtype=jnp.int32)
    inside = (positions >= my_offset) & (positions < my_offset + my_count * out_len)
    return jnp.where(inside[:, None], placed, text_embed[0])[None]


def solution(mesh):
    placed = (
        P(("section", "dp"), "tensor", None),
        P(),
        P(None, None, "tensor"),
        P("tensor"),
        P("tensor"),
        P("tensor", None),
        P(),
        P(None, "tensor"),
        P(("section", "dp"), None, "tensor"),
        P(),
        P(),
        P(),
    )
    return jax.shard_map(
        shards,
        mesh=mesh,
        in_specs=placed,
        out_specs=P(("section", "dp"), None, "tensor"),
        check_vma=False,
    )
```

profile of v0, /device:TPU:1, one launch (start us, length us, event | category | flops | bytes accessed | tf_op | source)
XLA Modules:
  0.0 450.3 jit_solution(15271659123102809501)
XLA Ops:
  6.5 1.5 fusion.16
  8.1 2.3 fusion.18
  10.5 11.4 %copy.19 = bf16[3200,3,384]{0,2,1:T(8,128)(2,1)} copy(bf16[3200,3,384]{2,0,1:T(8,128)(2,1)} %param.14) | data formatting | bytes 14745600 | tf_op args[2]
  21.8 82.5 %all-gather.5.cloned.1.call-done = bf16[1,1024,3200]{2,1,0:T(8,128)(2,1)} async-done(((bf16[1,128,3200]{2,1,0:T(8,128)(2,1)}), bf16[1,1024,3200]{2,1,0:T(8,128)(2,1)}) %all-gather.5.cloned.1.call-update) | async-done | bytes 6553616 | tf_op jit(solution)/shard_map/all_gather | solution.py:37
  104.4 13.3 %fusion.11 = f32[1,1024,1152]{2,1,0:T(8,128)S(1)} fusion(bf16[3200,1152]{0,1:T(8,128)(2,1)} %bitcast.55, bf16[1,1024,3200]{2,1,0:T(8,128)(2,1)} %all-gather.5.cloned.1.call-done), kind=kOutput, calls=%fused_computation.15 | convolution fusion | flops 7549747200 | bytes 18644992 | tf_op jit(solution)/shard_map/dot_general | solution.py:38
  118.0 1.7 copy-done.2
  119.8 16.8 %all-reduce = (f32[1,1024]{1,0:T(1,128)S(1)}, f32[1,1024]{1,0:T(1,128)S(1)}) all-reduce(f32[1,1024]{1,0:T(1,128)S(1)} %bitcast.61, f32[1,1024]{1,0:T(1,128)S(1)} %bitcast.60), channel_id=1, replica_groups=mesh['section'=8,'dp'=2,'tensor'=8] {'tensor'}, use_global_device_ids=true, to_apply=%region_3.0 | all-reduce | flops 2048 | bytes 16384 | tf_op jit(solution)/shard_map/psum | solution.py:44
  136.6 3.4 multiply_convert_fusion
  140.0 2.3 copy.21
  142.4 2.3 copy.22
  144.7 1.2 copy.20
  145.8 10.1 %fusion.33 = (f32[3,1024]{1,0:T(4,128)S(1)}, f32[3,1024,1024]{1,2,0:T(8,128)}) fusion(bf16[1024,3,128]{0,2,1:T(8,128)(2,1)} %bitcast.57, bf16[1024,3,128]{0,2,1:T(8,128)(2,1)} %bitcast.59), kind=kOutput, calls=%fused_computation.53 | convolution fusion | flops 814744576 | bytes 14168064 | tf_op jit(solution)/shard_map/sub | solution.py:61
  155.9 5.6 %fusion.20 = bf16[3,128,1024]{2,1,0:T(8,128)(2,1)S(1)} fusion(bf16[1024,3,128]{0,2,1:T(8,128)(2,1)S(1)} %bitcast.58, f32[3,1024,1024]{1,2,0:T(8,128)} %get-tuple-element.12, f32[3,1024]{1,0:T(4,128)S(1)} %get-tuple-element.11), kind=kOutput, calls=%fused_computation.30 | convolution fusion | flops 811991040 | bytes 14168064 | tf_op jit(solution)/shard_map/bhqk,bkhd->bqhd/dot_general | solution.py:62
  161.5 5.7 %fusion.8 = bf16[1024,1,3200]{2,0,1:T(8,128)(2,1)} fusion(bf16[1024,384]{0,1:T(8,128)(2,1)S(1)} %bitcast.65, bf16[384,3200]{1,0:T(8,128)(2,1)S(1)} %copy-done), kind=kOutput, calls=%fused_computation.12 | convolution fusion | flops 2519859200 | bytes 9797632 | tf_op jit(solution)/shard_map/dot_general | solution.py:67
  167.3 102.7 %reduce-scatter.2.cloned.1.call-done = bf16[128,1,3200]{2,0,1:T(8,128)(2,1)} async-done(((bf16[1024,1,3200]{2,0,1:T(8,128)(2,1)}), bf16[128,1,3200]{2,0,1:T(8,128)(2,1)}) %reduce-scatter.2.cloned.1.call-update) | async-done | bytes 819216 | tf_op jit(solution)/shard_map/reduce_scatter | solution.py:69
  270.0 2.3 fusion.19
  272.3 2.2 reshape.237
  274.5 1.5 copy.31
  276.0 3.2 reshape.238
  279.5 89.3 %all-gather.7.cloned.1.call-done = bf16[1,256,12800]{2,1,0:T(8,128)(2,1)} async-done(((bf16[1,32,12800]{2,1,0:T(8,128)(2,1)}), bf16[1,256,12800]{2,1,0:T(8,128)(2,1)}) %all-gather.7.cloned.1.call-update) | async-done | bytes 6553616 | tf_op jit(solution)/shard_map/all_gather | solution.py:87
  368.8 10.8 %fusion.21 = bf16[256,512]{1,0:T(8,128)(2,1)} fusion(bf16[12800,512]{1,0:T(8,128)(2,1)} %param.19, bf16[1,256,12800]{2,1,0:T(8,128)(2,1)} %all-gather.7.cloned.1.call-done), kind=kOutput, calls=%fused_computation.31 | convolution fusion | flops 3355574272 | bytes 19922944 | tf_op jit(solution)/shard_map/dot_general | solution.py:88
  379.9 0.7 dynamic_slice.10
  380.6 0.6 dynamic_slice.11
  384.8 0.6 gather_fusion
  386.0 0.7 iota_compare_fusion.2
  387.3 0.6 and_select_fusion
  387.9 40.4 %all-gather.9.cloned.1.call-done = bf16[4096,512]{1,0:T(8,128)(2,1)} async-done(((bf16[256,512]{1,0:T(8,128)(2,1)}), bf16[4096,512]{1,0:T(8,128)(2,1)}) %all-gather.9.cloned.1.call-update) | async-done | bytes 4194320 | tf_op jit(solution)/shard_map/all_gather | solution.py:106
  428.4 4.8 %reshape.240 = bf16[16,131072]{1,0:T(8,128)(2,1)} reshape(bf16[4096,512]{1,0:T(8,128)(2,1)} %all-gather.9.cloned.1.call-done) | data formatting | bytes 8388608 | tf_op jit(solution)/shard_map/reshape | solution.py:112
  433.2 3.0 convolution_convert_fusion
  436.2 1.3 reshape.241
  437.5 4.0 dynamic_update_slice.3
  441.5 2.2 fusion.24
  (40 shorter events, 3.0 us)
Async XLA Ops:
  6.5 155.0 %copy-start = (bf16[384,3200]{1,0:T(8,128)(2,1)S(1)}, bf16[384,3200]{1,0:T(8,128)(2,1)}, u32[]{:S(2)}) copy-start(bf16[384,3200]{1,0:T(8,128)(2,1)} %param.17) | copy-start | bytes 7372804
  6.5 97.8 %all-gather.5.cloned.1.call-start = ((), (), s32[]{:S(2)}) async-start(), calls=%async_computation.1 | async-start | bytes 7372800 | tf_op jit(solution)/shard_map/all_gather | solution.py:37
  10.4 259.6 %reduce-scatter.2.cloned.1.call-start = ((), (), s32[]{:S(2)}) async-start(), calls=%async_computation.2 | async-start | bytes 7372800 | tf_op jit(solution)/shard_map/reduce_scatter | solution.py:69
  117.6 2.1 copy-start.2
  117.6 19.0 %copy-start.6 = (f32[384]{0:T(512)S(1)}, f32[384]{0:T(512)}, u32[]{:S(2)}) copy-start(f32[384]{0:T(512)} %param.16) | copy-start | bytes 4612
  117.6 19.0 %copy-start.7 = (f32[384]{0:T(512)S(1)}, f32[384]{0:T(512)}, u32[]{:S(2)}) copy-start(f32[384]{0:T(512)} %param.15) | copy-start | bytes 4612
  145.8 10.1 %copy-start.4 = (bf16[1,1024,384]{1,2,0:T(8,128)(2,1)S(1)}, bf16[1,1024,384]{1,2,0:T(8,128)(2,1)}, u32[]{:S(2)}) copy-start(bf16[1,1024,384]{1,2,0:T(8,128)(2,1)} %copy.20) | copy-start | bytes 2359300
  167.2 102.8 %copy-start.3 = (bf16[1,128,3200]{2,1,0:T(8,128)(2,1)S(1)}, bf16[1,128,3200]{2,1,0:T(8,128)(2,1)}, u32[]{:S(2)}) copy-start(bf16[1,128,3200]{2,1,0:T(8,128)(2,1)} %param.12) | copy-start | bytes 2457604
  167.2 102.8 %copy-start.5 = (f32[3200]{0:T(1024)S(1)}, f32[3200]{0:T(1024)}, u32[]{:S(2)}) copy-start(f32[3200]{0:T(1024)} %param.18) | copy-start | bytes 38404
  167.2 201.6 %all-gather.7.cloned.1.call-start = ((), (), s32[]{:S(2)}) async-start(), calls=%async_computation.3 | async-start | bytes 7372800 | tf_op jit(solution)/shard_map/all_gather | solution.py:87
  279.2 100.5 %copy-start.8 = (s32[16]{0:T(128)S(1)}, s32[16]{0:T(128)}, u32[]{:S(2)}) copy-start(s32[16]{0:T(128)} %param.21) | copy-start | bytes 196
  279.2 102.0 %copy-start.9 = (s32[16]{0:T(128)S(1)}, s32[16]{0:T(128)}, u32[]{:S(2)}) copy-start(s32[16]{0:T(128)} %param.22) | copy-start | bytes 196
  279.2 105.6 %copy-start.1 = (s32[16]{0:T(128)S(1)}, s32[16]{0:T(128)}, u32[]{:S(2)}) copy-start(s32[16]{0:T(128)} %param.23) | copy-start | bytes 196
  279.3 149.1 %all-gather.9.cloned.1.call-start = ((), (), s32[]{:S(2)}) async-start(), calls=%async_computation.4 | async-start | bytes 4456448 | tf_op jit(solution)/shard_map/all_gather | solution.py:106
Sparse Core Ops, SparseCore 0:
  10.5 93.7 all-gather.4
  167.4 102.6 reduce-scatter.1
  279.3 89.4 all-gather.6
  379.8 48.5 all-gather.8
where the time goes:
time: 451 us; the launch traced here: 450 us
  waiting for transfers between devices  315 us (70%)
  matrix products  48.5 us (11%)
  local copies, waits for them, and re-layouts  38.6 us (9%)
  blocking collectives  16.8 us (4%)
  between operations  16.3 us (4%)
  other arithmetic  14.7 us (3%)
    reduce_scatter x1, waiting for transfers between devices, shards(): lax.psum_scatter(flat.reshape(rows_here * lax.axis_size('tensor'), tiles_...  103 us
    all_gather x1, waiting for transfers between devices, shards(): shard_rows = lax.all_gather(merged, 'tensor', axis=1, tiled=True)  89.3 us
    all_gather x1, waiting for transfers between devices, shards(): shard_rows = lax.all_gather(normed, 'tensor', axis=1, tiled=True)  82.5 us
    all_gather x1, waiting for transfers between devices, shards(): lax.all_gather(projected, ('section', 'dp'), axis=0, tiled=True)  40.4 us
    psum x1, blocking collectives, shards(): lax.psum((jnp.sum(query_part * query_part, axis=-1), jnp.sum(key_part * k...  16.8 us
    dot_general x1, matrix products, shards(): jnp.dot(shard_rows.reshape(-1, width_d), w_flat, preferred_element_type=j...  13.3 us
    unnamed x21, local copies, waits for them, and re-layouts  13.2 us
    dot_general x1, matrix products, shards(): jnp.dot(shard_rows.reshape(-1, shard_rows.shape[2]), w_proj, preferred_el...  10.8 us
  transfers between devices with their start and end apart: 4, of which 4 were waited for; matrix products, arithmetic and copies ran while one was open for 4% of the time, Pallas kernels for 0%

commit v1 on v0

v1 whole, which is shorter than its diff:
```python
import functools

import jax
import jax.numpy as jnp
from jax import lax
from jax.experimental import pallas as pl
from jax.experimental.pallas import tpu as pltpu
from jax.sharding import PartitionSpec as P

D = 3200
HEADS = 24
HD = 128
CH = 128
LH = 3
LW = 384
F32 = jnp.float32
BF16 = jnp.bfloat16
MESH = pl.DeviceIdType.MESH
EPS = 1e-06
VMEM = pltpu.VMEM
PARAMS = dict(has_side_effects=True, vmem_limit_bytes=60 * 1024 * 1024)

O0, X0, O1, OM, X1, XM, O2, X2 = range(8)

GATHER = (
    (O0, 0, 64, "x", X0),
    (O0, 0, 64, "p", OM),
    (O0, 0, 64, "m", O1),
    (O0, 64, 64, "p", OM),
    (O0, 64, 64, "m", O1),
    (O0, 64, 64, "x", X0),
    (OM, 0, 32, "p", O2),
    (O1, 32, 32, "m", O2),
    (X0, 0, 64, "p", XM),
    (X0, 0, 64, "m", X1),
    (XM, 0, 32, "p", X2),
    (X1, 32, 32, "m", X2),
    (OM, 64, 32, "p", O2),
    (O1, 96, 32, "m", O2),
    (OM, 64, 64, "x", XM),
    (O1, 64, 64, "x", X1),
    (O2, 64, 32, "x", X2),
    (O2, 96, 32, "x", X2),
)

SCATTER = (
    (X2, 0, 32, "p", X1, 0),
    (X2, 32, 32, "m", XM, 32),
    (X2, 64, 64, "x", O2, 64),
    (O2, 0, 32, "p", O1, 128),
    (O2, 32, 32, "m", OM, 160),
    (X1, 64, 64, "x", O1, 192),
    (XM, 64, 64, "x", OM, 256),
    (X1, 0, 64, "p", X0, 320),
    (XM, 0, 64, "m", X0, 384),
    (O1, 0, 64, "p", O0, 448),
    (OM, 0, 64, "m", O0, 512),
    (O2, 64, 32, "p", O1, 576),
    (O2, 96, 32, "m", OM, 608),
    (X0, 64, 64, "x", O0, 640),
    (X0, 0, 64, "x", O0, 704),
    (O1, 64, 64, "p", O0, 768),
    (OM, 64, 64, "m", O0, 832),
)
LAND_ROWS = 896


def where_am_i():
    t = lax.axis_index("tensor")
    xh = t // 4
    y = lax.rem(t, 4)
    return t, xh, y


def directions():
    _, xh, y = where_am_i()
    return {
        "p": {"tensor": xh * 4 + lax.rem(y + 1, 4)},
        "m": {"tensor": xh * 4 + lax.rem(y + 3, 4)},
        "x": {"tensor": (1 - xh) * 4 + y},
    }


def slot_chunks():
    _, xh, y = where_am_i()
    near, far = xh * 4, (1 - xh) * 4
    up, down, opposite = lax.rem(y + 1, 4), lax.rem(y + 3, 4), lax.rem(y + 2, 4)
    return (near + y, far + y, near + up, near + down, far + up, far + down, near + opposite, far + opposite)


def gather_copies(buf, send, recv):
    where = directions()
    return [
        pltpu.make_async_remote_copy(
            src_ref=buf.at[src, pl.ds(row, rows)],
            dst_ref=buf.at[dst, pl.ds(row, rows)],
            send_sem=send.at[i],
            recv_sem=recv.at[i],
            device_id=where[way],
            device_id_type=MESH,
        )
        for i, (src, row, rows, way, dst) in enumerate(GATHER)
    ]


def scatter_copies(buf, land, send, recv):
    where = directions()
    return [
        pltpu.make_async_remote_copy(
            src_ref=buf.at[src, pl.ds(row, rows)],
            dst_ref=land.at[pl.ds(place, rows)],
            send_sem=send.at[i],
            recv_sem=recv.at[i],
            device_id=where[way],
            device_id_type=MESH,
        )
        for i, (src, row, rows, way, dst, place) in enumerate(SCATTER)
    ]


def merge_order(row0, rows):
    r = lax.broadcasted_iota(jnp.int32, (rows, CH), 0) + row0
    c = lax.broadcasted_iota(jnp.int32, (rows, CH), 1)
    a, b, i, j = r // 64, (r // 32) % 2, (r // 16) % 2, r % 16
    return ((2 * i + a) * 32 + 2 * j + b == c).astype(F32).astype(BF16)


def qkv_kernel(patches, gain, w_hbm, q_gain, k_gain, q_out, k_out, v_out, xg, w, qk, sums, w_sem, send, recv, s_send, s_recv):
    t, _, _ = where_am_i()
    chunk_of = slot_chunks()
    w_copies = [pltpu.make_async_copy(w_hbm.at[j], w.at[j], w_sem.at[j]) for j in range(3)]
    for c in w_copies:
        c.start()
    barrier = pltpu.get_barrier_semaphore()
    for k in range(1, 8):
        pl.semaphore_signal(barrier, inc=1, device_id={"tensor": lax.rem(t + k, 8)}, device_id_type=MESH)

    def norm(row0):
        x = jnp.dot(merge_order(row0, 32), patches[...], preferred_element_type=F32)
        scale = lax.rsqrt(jnp.mean(x * x, axis=-1, keepdims=True) + EPS)
        xg[O0, pl.ds(row0, 32)] = (x * scale * gain[...]).astype(BF16)

    cp = gather_copies(xg, send, recv)
    norm(0)
    norm(32)
    pl.semaphore_wait(barrier, 7)
    for i in (0, 1, 2):
        cp[i].start()
    norm(64)
    norm(96)
    for i in (3, 4, 5):
        cp[i].start()
    for c in w_copies:
        c.wait()

    def after(done, *then):
        cp[done].wait_recv()
        for i in then:
            cp[i].start()

    def project(g):
        x = xg[2 * g : 2 * g + 2].reshape(2 * CH, D)
        rows = pl.ds(2 * g * CH, 2 * CH)
        for j in range(2):
            part = jnp.dot(x, w[j], preferred_element_type=F32)
            qk[j, rows] = part
            for u in range(2):
                p = part[u * CH : (u + 1) * CH]
                sq = p * p
                sq = sq[:, :HD] + sq[:, HD : 2 * HD] + sq[:, 2 * HD :]
                row = jnp.sum(jnp.transpose(sq), axis=0, keepdims=True)
                sums[t, chunk_of[2 * g + u], :, j * HD : (j + 1) * HD] = row
        part = jnp.dot(x, w[2], preferred_element_type=F32).astype(BF16)
        for h in range(LH):
            v_out[h, rows] = part[:, h * HD : (h + 1) * HD]

    after(1, 6)
    after(2, 7)
    after(0, 8, 9)
    after(3, 12, 14)
    after(4, 13, 15)
    after(5)
    project(0)
    after(8, 10)
    after(9, 11)
    after(12, 16)
    after(13, 17)
    project(1)
    after(14)
    after(15)
    project(2)
    for i in (6, 7, 10, 11, 16, 17):
        after(i)
    project(3)

    s_copies = [
        pltpu.make_async_remote_copy(
            src_ref=sums.at[t],
            dst_ref=sums.at[t],
            send_sem=s_send.at[k],
            recv_sem=s_recv.at[k],
            device_id={"tensor": lax.rem(t + k, 8)},
            device_id_type=MESH,
        )
        for k in range(1, 8)
    ]
    for c in s_copies:
        c.start()
    for c in cp:
        c.wait_send()
    for k in range(1, 8):
        pltpu.make_async_remote_copy(
            src_ref=sums.at[lax.rem(t + 8 - k, 8)],
            dst_ref=sums.at[lax.rem(t + 8 - k, 8)],
            send_sem=s_send.at[k],
            recv_sem=s_recv.at[k],
            device_id={"tensor": lax.rem(t + k, 8)},
            device_id_type=MESH,
        ).wait_recv()
    for slot in range(8):
        total = sums[0, chunk_of[slot]]
        for other in range(1, 8):
            total = total + sums[other, chunk_of[slot]]
        scale = lax.rsqrt(total / (HEADS * HD) + EPS)
        rows = pl.ds(slot * CH, CH)
        for j, (out, g, extra) in enumerate(((q_out, q_gain, HD**-0.5), (k_out, k_gain, 1.0))):
            col = jnp.transpose(jnp.broadcast_to(scale[:, j * HD : (j + 1) * HD], (CH, HD))) * extra
            for h in range(LH):
                lanes = slice(h * HD, (h + 1) * HD)
                out[h, rows] = (qk[j, rows, lanes] * col * g[:, lanes]).astype(BF16)
    for c in s_copies:
        c.wait_send()


def encode_kernel(
    q, k, v, patches, layer_scale, wo_hbm, wp_hbm, counts, slots, feats,
    wo, wp, ob, land, xg, mixed, proj, pieces, picked, arrive,
    w_sem, r_send, r_recv, send, recv, a_send, a_recv, b_send, b_recv,
):
    chunk_of = slot_chunks()
    section = lax.axis_index("section")
    dp = lax.axis_index("dp")
    me = section * 2 + dp
    wo_copy = pltpu.make_async_copy(wo_hbm, wo, w_sem.at[0])
    wp_copy = pltpu.make_async_copy(wp_hbm, wp, w_sem.at[1])
    wo_copy.start()
    wp_copy.start()
    barrier = pltpu.get_barrier_semaphore()
    where = directions()
    for way in ("p", "m", "x"):
        pl.semaphore_signal(barrier, inc=1, device_id=where[way], device_id_type=MESH)

    def group(index):
        return {"section": index // 2, "dp": lax.rem(index, 2)}

    for n in range(1, 16):
        pl.semaphore_signal(barrier, inc=1, device_id=group(lax.rem(me + n, 16)), device_id_type=MESH)
    rc = scatter_copies(ob, land, r_send, r_recv)
    gc = gather_copies(xg, send, recv)

    def attend(first):
        def one(step, _):
            h = step % LH
            r0 = pl.multiple_of((step // LH) * CH, CH)
            rows = pl.ds(first * CH + r0, CH)
            scores = lax.dot_general(q[h, rows], k[h], (((1,), (1,)), ((), ())), preferred_element_type=F32)
            e = jnp.exp(scores - jnp.max(scores, axis=-1, keepdims=True))
            total = jnp.sum(e, axis=-1, keepdims=True)
            part = jnp.dot(e.astype(BF16), v[h], preferred_element_type=F32)
            mixed[h, pl.ds(r0, CH)] = (part / total).astype(BF16)
            return _

        lax.fori_loop(0, 2 * LH, one, 0)

        both = jnp.concatenate([mixed[h] for h in range(LH)], axis=1)
        for n0 in range(0, D, 640):
            part = jnp.dot(both, wo[:, n0 : n0 + 640], preferred_element_type=F32).astype(BF16)
            ob[first, :, n0 : n0 + 640] = part[:CH]
            ob[first + 1, :, n0 : n0 + 640] = part[CH:]

    def add(i):
        rc[i].wait_recv()
        _, row, rows, _, dst, place = SCATTER[i]
        for r in range(0, rows, 32):
            total = ob[dst, row + r : row + r + 32].astype(F32) + land[place + r : place + r + 32].astype(F32)
            ob[dst, row + r : row + r + 32] = total.astype(BF16)

    wo_copy.wait()
    attend(O2)
    pl.semaphore_wait(barrier, 18)
    for i in (0, 1, 2, 3, 4):
        rc[i].start()
    attend(X1)
    for i in (5, 6):
        rc[i].start()
    add(0)
    rc[7].start()
    add(1)
    rc[8].start()
    attend(O1)
    add(3)
    rc[9].start()
    add(4)
    rc[10].start()
    add(2)
    rc[11].start()
    rc[12].start()
    attend(O0)
    rc[13].start()
    add(7)
    add(8)
    rc[14].start()
    add(5)
    add(11)
    rc[15].start()
    add(6)
    add(12)
    rc[16].start()
    add(9)
    add(10)
    add(13)

    def encode(row0):
        base = jnp.dot(merge_order(row0, 32), patches[...], preferred_element_type=F32)
        branch = ob[O0, row0 : row0 + 32].astype(F32)
        xg[O0, pl.ds(row0, 32)] = (base + layer_scale[...] * branch).astype(BF16)

    add(14)
    encode(0)
    encode(32)
    for i in (0, 1, 2):
        gc[i].start()
    add(15)
    add(16)
    encode(64)
    encode(96)
    for i in (3, 4, 5):
        gc[i].start()
    for c in rc:
        c.wait_send()

    def after(done, *then):
        gc[done].wait_recv()
        for i in then:
            gc[i].start()

    def project(ab):
        x = xg[:, ab * 32 : (ab + 1) * 32, :].reshape(8 * 32, D)
        return jnp.dot(x, wp[ab * D : (ab + 1) * D, :], preferred_element_type=F32)

    after(1, 6)
    after(2, 7)
    after(0, 8, 9)
    after(3, 12, 14)
    after(4, 13, 15)
    after(5)
    after(8, 10)
    after(9, 11)
    after(12, 16)
    after(13, 17)
    wp_copy.wait()
    for i in (6, 7, 10, 11):
        after(i)
    total = project(0) + project(1)
    for i in (14, 15, 16, 17):
        after(i)
    total = (total + project(2) + project(3)).astype(BF16)
    for slot in range(8):
        proj[pl.ds(2 * chunk_of[slot], 2)] = total[slot * 32 : (slot + 1) * 32].reshape(2, 16, 512)
    for c in gc:
        c.wait_send()

    first = [
        pltpu.make_async_remote_copy(
            src_ref=proj.at[lax.rem(me + n, 16)],
            dst_ref=pieces.at[me],
            send_sem=a_send.at[n],
            recv_sem=a_recv.at[n],
            device_id=group(lax.rem(me + n, 16)),
            device_id_type=MESH,
        )
        for n in range(1, 16)
    ]
    for c in first:
        c.start()
    pieces[me] = proj[me]
    for n in range(1, 16):
        source = lax.rem(me + 16 - n, 16)
        pltpu.make_async_remote_copy(
            src_ref=pieces.at[source],
            dst_ref=pieces.at[source],
            send_sem=a_send.at[n],
            recv_sem=a_recv.at[n],
            device_id=group(lax.rem(me + n, 16)),
            device_id_type=MESH,
        ).wait_recv()
    start = jnp.int32(0)
    for g in range(16):
        for s in range(2):
            tile = slots[jnp.minimum(start + s, 15)]
            picked[g, s] = pieces[tile]
        start = start + counts[g]
    second = [
        pltpu.make_async_remote_copy(
            src_ref=picked.at[lax.rem(me + n, 16)],
            dst_ref=arrive.at[me],
            send_sem=b_send.at[n],
            recv_sem=b_recv.at[n],
            device_id=group(lax.rem(me + n, 16)),
            device_id_type=MESH,
        )
        for n in range(1, 16)
    ]
    for c in second:
        c.start()
    arrive[me] = picked[me]
    for n in range(1, 16):
        source = lax.rem(me + 16 - n, 16)
        pltpu.make_async_remote_copy(
            src_ref=arrive.at[source],
            dst_ref=arrive.at[source],
            send_sem=b_send.at[n],
            recv_sem=b_recv.at[n],
            device_id=group(lax.rem(me + n, 16)),
            device_id_type=MESH,
        ).wait_recv()
    for n in range(16):
        for s in range(2):
            feats[s * 256 + n * 16 : s * 256 + n * 16 + 16, :] = arrive[n, s]
    for c in first:
        c.wait_send()
    for c in second:
        c.wait_send()


def place_kernel(feats, text, counts, offsets, out):
    me = lax.axis_index("section") * 2 + lax.axis_index("dp")
    rows = counts[me] * 256
    offset = offsets[me]
    seq = text.shape[0]
    for r0 in range(0, seq, 256):
        r = lax.broadcasted_iota(jnp.int32, (256, 512), 0) + r0 - offset
        c = lax.broadcasted_iota(jnp.int32, (256, 512), 1)
        pick = (r == c).astype(F32).astype(BF16)
        moved = jnp.dot(pick, feats[...], preferred_element_type=F32)
        inside = (r >= 0) & (r < rows)
        out[r0 : r0 + 256, :] = jnp.where(inside, moved, text[r0 : r0 + 256, :].astype(F32)).astype(BF16)


def spec(space):
    return pl.BlockSpec(memory_space=space)


def shards(
    patches,
    norm_gain,
    w_qkv,
    q_gain,
    k_gain,
    w_out,
    layer_scale,
    w_proj,
    text_embed,
    tile_counts,
    image_offsets,
    tile_slots,
):
    chunk = patches[0]
    heads = jax.ShapeDtypeStruct((LH, 8 * CH, HD), BF16)
    dma = pltpu.SemaphoreType.DMA
    q, k, v = pl.pallas_call(
        qkv_kernel,
        out_shape=(heads, heads, heads),
        in_specs=[spec(VMEM), spec(VMEM), spec(pl.ANY), spec(VMEM), spec(VMEM)],
        out_specs=(spec(VMEM), spec(VMEM), spec(VMEM)),
        scratch_shapes=[
            VMEM((8, CH, D), BF16),
            VMEM((3, D, LW), BF16),
            VMEM((2, 8 * CH, LW), F32),
            VMEM((8, 8, 1, 2 * HD), F32),
            dma((3,)),
            dma((18,)),
            dma((18,)),
            dma((8,)),
            dma((8,)),
        ],
        compiler_params=pltpu.CompilerParams(collective_id=0, **PARAMS),
        name="qkv",
    )(chunk, norm_gain.reshape(1, D), w_qkv.transpose(1, 0, 2), q_gain.reshape(1, LW), k_gain.reshape(1, LW))
    smem = pltpu.SMEM
    feats = pl.pallas_call(
        encode_kernel,
        out_shape=jax.ShapeDtypeStruct((512, 512), BF16),
        in_specs=[spec(VMEM)] * 5 + [spec(pl.ANY)] * 2 + [spec(smem)] * 2,
        out_specs=spec(VMEM),
        scratch_shapes=[
            VMEM((LW, D), BF16),
            VMEM((4 * D, 512), BF16),
            VMEM((8, CH, D), BF16),
            VMEM((LAND_ROWS, D), BF16),
            VMEM((8, CH, D), BF16),
            VMEM((LH, 2 * CH, HD), BF16),
            VMEM((16, 16, 512), BF16),
            VMEM((16, 16, 512), BF16),
            VMEM((16, 2, 16, 512), BF16),
            VMEM((16, 2, 16, 512), BF16),
            dma((2,)),
            dma((17,)),
            dma((17,)),
            dma((18,)),
            dma((18,)),
            dma((16,)),
            dma((16,)),
            dma((16,)),
            dma((16,)),
        ],
        compiler_params=pltpu.CompilerParams(collective_id=1, **PARAMS),
        name="encode",
    )(q, k, v, chunk, layer_scale.reshape(1, D), w_out, w_proj, tile_counts, tile_slots)
    out = pl.pallas_call(
        place_kernel,
        out_shape=jax.ShapeDtypeStruct(text_embed.shape[1:], BF16),
        in_specs=[spec(VMEM)] * 2 + [spec(smem)] * 2,
        out_specs=spec(VMEM),
        compiler_params=pltpu.CompilerParams(vmem_limit_bytes=32 * 1024 * 1024),
        name="place",
    )(feats, text_embed[0], tile_counts, image_offsets)
    return out[None]


def solution(mesh):
    placed = (
        P(("section", "dp"), "tensor", None),
        P(),
        P(None, None, "tensor"),
        P("tensor"),
        P("tensor"),
        P("tensor", None),
        P(),
        P(None, "tensor"),
        P(("section", "dp"), None, "tensor"),
        P(),
        P(),
        P(),
    )
    return jax.shard_map(
        shards,
        mesh=mesh,
        in_specs=placed,
        out_specs=P(("section", "dp"), None, "tensor"),
        check_vma=False,
    )
```

time: 451 us -> 192 us (0.43)
  waiting for transfers between devices: 315 us -> 0 us
  Pallas kernels: 0 us -> 185 us
  matrix products: 48.5 us -> 0 us
  local copies, waits for them, and re-layouts: 38.6 us -> 6.23 us
  blocking collectives: 16.8 us -> 0 us
  between operations: 16.3 us -> 0.08 us
  other arithmetic: 14.7 us -> 0 us
    all_gather x3 -> x0, waiting for transfers between devices: 212 us -> none  [the longest x1 89.3 us: shards(): shard_rows = lax.all_gather(merged, 'tensor', axis=1, tiled=True)]
    pallas_call x0 -> x3, Pallas kernels: none -> 185 us  [the longest x1 122 us: shards(): pl.pallas_call(encode_kernel, out_shape=jax.ShapeDtypeStruct((512, 512),...]
    reduce_scatter x1 -> x0, waiting for transfers between devices: 103 us -> none  [shards(): lax.psum_scatter(flat.reshape(rows_here * lax.axis_size('tensor'), tiles_...]
    dot_general x5 -> x0, matrix products: 38.4 us -> none  [the longest x1 13.3 us: shards(): jnp.dot(shard_rows.reshape(-1, width_d), w_flat, preferred_element_type=j...]
    psum x1 -> x0, blocking collectives: 16.8 us -> none  [shards(): lax.psum((jnp.sum(query_part * query_part, axis=-1), jnp.sum(key_part * k...]
    unnamed x21 -> x8, local copies, waits for them, and re-layouts: 13.2 us -> 1.05 us
    sub x1 -> x0, matrix products: 10.1 us -> none  [shards(): weights = jax.nn.softmax(scores, axis=-1).astype(jnp.bfloat16)]
    convert_element_type x3 -> x0, other arithmetic: 7.99 us -> none  [the longest x1 3.4 us: shards(): (key_part * lax.rsqrt(key_sq[..., None] / full_width + 1e-06) * k_gain).a...]
  transfers between devices with their start and end apart: 4 -> 0, of which waited for: 4 -> 0; matrix products, arithmetic and copies ran while one was open for 4% -> 0% of each run, Pallas kernels for 0% -> 0%
where the time goes in v1:
time: 192 us; the launch traced here: 191 us
  Pallas kernels  185 us (96%)
  local copies, waits for them, and re-layouts  6.23 us (3%)
    pallas_call x1, Pallas kernels, shards(): pl.pallas_call(encode_kernel, out_shape=jax.ShapeDtypeStruct((512, 512),...  122 us
    pallas_call x1, Pallas kernels, shards(): pl.pallas_call(qkv_kernel, out_shape=(heads, heads, heads), in_specs=[spe...  60.8 us

profile of v1, /device:TPU:1, one launch (start us, length us, event | category | flops | bytes accessed | tf_op | source)
XLA Modules:
  0.0 191.2 jit_solution(1297079822534832063)
XLA Ops:
  0.0 1.3 reshape.13.q_gain
  1.3 1.3 reshape.14.k_gain
  2.5 1.3 reshape.12.gain
  3.9 1.3 reshape.15.layer_scale
  5.2 60.8 %qkv.1 = (bf16[3,1024,128]{2,1,0:T(8,128)(2,1)}, bf16[3,1024,128]{2,1,0:T(8,128)(2,1)}, bf16[3,1024,128]{2,1,0:T(8,128)(2,1)}) custom-call(bf16[128,3200]{1,0:T(8,128)(2,1)} %bitcast.6, f32[1,3200]{1,0:T(1,128)} %reshape.12.gain, bf16[3,3200,384]{2,1,0:T(8,128)(2,1)} %bitcast.5, f32[1,384]{1,0:T(1,128)} %reshape.13.q_gain, f32[1,384]{1,0:T(1,128)} %reshape.14.k_gain), custom_call_target="tpu_custom_call" | custom-call | tf_op jit(solution)/shard_map/qkv/pallas_call | solution.py:471
  66.0 0.0 copy-start.1
  66.0 0.0 copy-start.2
  66.1 0.0 copy-start.3
  66.1 122.0 %encode.1.feats = bf16[512,512]{1,0:T(8,128)(2,1)} custom-call(bf16[3,1024,128]{2,1,0:T(8,128)(2,1)} %get-tuple-element.8.q, bf16[3,1024,128]{2,1,0:T(8,128)(2,1)} %get-tuple-element.9.k, bf16[3,1024,128]{2,1,0:T(8,128)(2,1)} %get-tuple-element.10.v, bf16[128,3200]{1,0:T(8,128)(2,1)} %bitcast.7, f32[1,3200]{1,0:T(1,128)} %reshape.15.layer_scale, ...), custom_call_target="tpu_custom_call" | custom-call | tf_op jit(solution)/shard_map/encode/pallas_call | solution.py:491
  188.1 0.0 copy-done.1
  188.1 0.0 copy-done.2
  188.1 0.0 copy-done.3
  188.1 0.0 copy-start
  188.1 1.0 copy-done
  189.2 2.0 %place.1 = bf16[768,512]{1,0:T(8,128)(2,1)} custom-call(bf16[512,512]{1,0:T(8,128)(2,1)S(1)} %copy-done, bf16[768,512]{1,0:T(8,128)(2,1)S(1)} %bitcast.4, s32[16]{0:T(128)S(1)} %copy-done.2, s32[16]{0:T(128)S(1)} %copy-done.3), custom_call_target="tpu_custom_call" | custom-call | tf_op jit(solution)/shard_map/place/pallas_call | solution.py:520
Async XLA Ops:
  66.0 122.1 %copy-start.1 = (bf16[1,768,512]{2,1,0:T(8,128)(2,1)S(1)}, bf16[1,768,512]{2,1,0:T(8,128)(2,1)}, u32[]{:S(2)}) copy-start(bf16[1,768,512]{2,1,0:T(8,128)(2,1)} %param.20) | copy-start | bytes 2359300
  66.0 122.1 %copy-start.2 = (s32[16]{0:T(128)S(1)}, s32[16]{0:T(128)}, u32[]{:S(2)}) copy-start(s32[16]{0:T(128)} %counts.3) | copy-start | bytes 196
  66.1 122.1 %copy-start.3 = (s32[16]{0:T(128)S(1)}, s32[16]{0:T(128)}, u32[]{:S(2)}) copy-start(s32[16]{0:T(128)} %offsets.1) | copy-start | bytes 196
  188.1 1.0 copy-start

commit v2 on v0

v2 whole, which is shorter than its diff:
```python
import jax
import jax.numpy as jnp
from jax import lax
from jax.experimental import pallas as pl
from jax.experimental.pallas import tpu as pltpu
from jax.sharding import PartitionSpec as P

D = 3200
HEADS = 24
HD = 128
CH = 128
LH = 3
LW = 384
F32 = jnp.float32
BF16 = jnp.bfloat16
MESH = pl.DeviceIdType.MESH
EPS = 1e-06
VMEM = pltpu.VMEM
PARAMS = dict(has_side_effects=True, vmem_limit_bytes=62 * 1024 * 1024)

O0, X0, O1, OM, X1, XM, O2, X2 = range(8)
N2, N1, NM, N0 = range(4)

GATHER = (
    (O0, 0, 80, "x", X0),
    (O0, 0, 80, "p", OM),
    (O0, 0, 80, "m", O1),
    (O0, 80, 48, "p", OM),
    (O0, 80, 48, "m", O1),
    (O0, 80, 48, "x", X0),
    (OM, 0, 48, "p", O2),
    (O1, 48, 32, "m", O2),
    (X0, 0, 80, "p", XM),
    (X0, 0, 80, "m", X1),
    (XM, 0, 48, "p", X2),
    (X1, 48, 32, "m", X2),
    (OM, 80, 16, "p", O2),
    (O1, 96, 32, "m", O2),
    (OM, 80, 48, "x", XM),
    (O1, 80, 48, "x", X1),
    (O2, 80, 16, "x", X2),
    (O2, 96, 32, "x", X2),
)

SCATTER = tuple(
    copy
    for b in (0, 64)
    for copy in (
        (N2, b, "p", N1),
        (N2, b + 32, "m", NM),
        (N1, b + 32, "p", N0),
        (N1, b, "p", N0),
        (NM, b, "m", N0),
        (NM, b + 32, "m", N0),
    )
)

SPREAD = tuple(
    copy
    for b in (0, 64)
    for copy in ((N0, b, 64, "p", NM), (N0, b, 64, "m", N1), (NM, b, 32, "p", N2), (N1, b + 32, 32, "m", N2))
)

SETS = ((48, 32), (400, 208), (400, 208), (400, 208), (400, 208))
WEIGHTS = ((0, 0, "u"), (0, 0, "d"), (0, 0, "c"), (-2, 1, "u"), (-2, 0, "c"), (2, 2, "d"), (2, 0, "c"), (4, 1, "c"), (4, 2, "c"))


def where_am_i():
    t = lax.axis_index("tensor")
    return t, t // 4, lax.rem(t, 4)


def directions():
    _, xh, y = where_am_i()
    section = lax.axis_index("section")
    return {
        "p": {"tensor": xh * 4 + lax.rem(y + 1, 4)},
        "m": {"tensor": xh * 4 + lax.rem(y + 3, 4)},
        "x": {"tensor": (1 - xh) * 4 + y},
        "cross": {"dp": 1 - lax.axis_index("dp"), "tensor": (1 - xh) * 4 + y},
        "u": {"section": lax.rem(section + 2, 8)},
        "d": {"section": lax.rem(section + 6, 8)},
        "c": {"section": section + 1 - 2 * lax.rem(section, 2)},
    }


def slot_chunks():
    _, xh, y = where_am_i()
    near, far = xh * 4, (1 - xh) * 4
    up, down, opposite = lax.rem(y + 1, 4), lax.rem(y + 3, 4), lax.rem(y + 2, 4)
    return (near + y, far + y, near + up, near + down, far + up, far + down, near + opposite, far + opposite)


def remote(src, dst, send, recv, target):
    return pltpu.make_async_remote_copy(
        src_ref=src, dst_ref=dst, send_sem=send, recv_sem=recv, device_id=target, device_id_type=MESH
    )


def table_copies(table, buf, send, recv):
    where = directions()
    return [
        remote(buf.at[src, pl.ds(row, rows)], buf.at[dst, pl.ds(row, rows)], send.at[i], recv.at[i], where[way])
        for i, (src, row, rows, way, dst) in enumerate(table)
    ]


def weight_copies(number, source, buf, base, send, recv):
    rows, first = SETS[number]
    section = lax.axis_index("section")
    where = directions()

    def part(ref, offset, which):
        start = base + lax.rem(section + 8 + offset, 8) * rows
        start, count = ((start, rows), (start, first), (start + first, rows - first))[which]
        return ref.at[pl.ds(pl.multiple_of(start, 16), count)]

    copies = [remote(part(source, 0, 0), part(buf, 0, 0), send.at[number, 0], recv.at[number, 0], where["cross"])]
    for i, (offset, which, way) in enumerate(WEIGHTS):
        there = part(buf, offset, which)
        copies.append(remote(there, there, send.at[number, i + 1], recv.at[number, i + 1], where[way]))
    return copies


def merge_order(row0, rows):
    r = lax.broadcasted_iota(jnp.int32, (rows, CH), 0) + row0
    c = lax.broadcasted_iota(jnp.int32, (rows, CH), 1)
    a, b, i, j = r // 64, (r // 32) % 2, (r // 16) % 2, r % 16
    return ((2 * i + a) * 32 + 2 * j + b == c).astype(F32).astype(BF16)


def encode_kernel(
    patches, gain, w_hbm, q_gain, k_gain, layer_scale, wo_hbm, wp_hbm, counts, slots, feats,
    xg, w, qk, sums, q, k, v, wo, wp, mix, far, ob, proj, pieces, picked, arrive,
    w_sem, g_send, g_recv, s_send, s_recv, x_send, x_recv, m_send, m_recv, r_send, r_recv, e_send, e_recv,
    a_send, a_recv, b_send, b_recv,
):
    t, xh, y = where_am_i()
    opp = (1 - xh) * 4 + y
    chunk_of = slot_chunks()
    me = lax.axis_index("section") * 2 + lax.axis_index("dp")

    def group(index, tensor):
        return {"section": index // 2, "dp": lax.rem(index, 2), "tensor": tensor}

    w_copies = [pltpu.make_async_copy(w_hbm.at[j], w.at[j], w_sem.at[j]) for j in range(3)]
    own_copies = [
        pltpu.make_async_copy(wo_hbm, wo.at[0], w_sem.at[3]),
        pltpu.make_async_copy(wp_hbm, wp.at[0], w_sem.at[4]),
    ]
    for c in w_copies + own_copies:
        c.start()
    barrier = pltpu.get_barrier_semaphore()
    for n in range(1, 8):
        pl.semaphore_signal(barrier, inc=1, device_id={"tensor": lax.rem(t + n, 8)}, device_id_type=MESH)
    for n in range(1, 16):
        for tensor in (t, opp):
            target = group(lax.rem(me + n, 16), tensor)
            pl.semaphore_signal(barrier, inc=1, device_id=target, device_id_type=MESH)

    def norm(row0, rows):
        x = jnp.dot(merge_order(row0, rows), patches[...], preferred_element_type=F32)
        scale = lax.rsqrt(jnp.mean(x * x, axis=-1, keepdims=True) + EPS)
        xg[O0, pl.ds(row0, rows)] = (x * scale * gain[...].reshape(1, D)).astype(BF16)

    gc = table_copies(GATHER, xg, g_send, g_recv)
    wc = [weight_copies(0, wo_hbm, wo.at[1], 0, x_send, x_recv)]
    wc += [weight_copies(1 + ab, wp_hbm, wp.at[1], ab * D, x_send, x_recv) for ab in range(4)]

    def weights_cross(n):
        wc[n][0].start()

    def weights_turn(n):
        wc[n][0].wait_recv()
        for i in (1, 2, 3):
            wc[n][i].start()

    def weights_forward(n):
        wc[n][1].wait_recv()
        wc[n][4].start()
        wc[n][5].start()
        wc[n][2].wait_recv()
        wc[n][6].start()
        wc[n][7].start()

    def weights_last(n):
        wc[n][4].wait_recv()
        wc[n][8].start()
        wc[n][6].wait_recv()
        wc[n][9].start()

    def weights_here(n):
        for i in (3, 5, 7, 8, 9):
            wc[n][i].wait_recv()

    norm(0, 32)
    norm(32, 32)
    norm(64, 16)
    pl.semaphore_wait(barrier, 37)
    for i in (0, 1, 2):
        gc[i].start()
    weights_cross(0)
    norm(80, 16)
    norm(96, 32)
    for i in (3, 4, 5):
        gc[i].start()
    for c in w_copies:
        c.wait()

    def after(done, *then):
        gc[done].wait_recv()
        for i in then:
            gc[i].start()

    def project_qkv(g):
        x = xg[2 * g : 2 * g + 2].reshape(2 * CH, D)
        rows = pl.ds(2 * g * CH, 2 * CH)
        for j in range(2):
            part = jnp.dot(x, w[j], preferred_element_type=F32)
            qk[j, rows] = part
            for u in range(2):
                p = part[u * CH : (u + 1) * CH]
                sq = p * p
                sq = sq[:, :HD] + sq[:, HD : 2 * HD] + sq[:, 2 * HD :]
                row = jnp.sum(jnp.transpose(sq), axis=0, keepdims=True)
                sums[t, chunk_of[2 * g + u], :, j * HD : (j + 1) * HD] = row
        part = jnp.dot(x, w[2], preferred_element_type=F32).astype(BF16)
        for h in range(LH):
            v[h, rows] = part[:, h * HD : (h + 1) * HD]

    after(1, 6)
    after(2, 7)
    after(0, 8, 9)
    after(3, 12, 14)
    after(4, 13, 15)
    after(5)
    project_qkv(0)
    after(8, 10)
    after(9, 11)
    after(12, 16)
    after(13, 17)
    weights_turn(0)
    weights_cross(1)
    project_qkv(1)
    weights_forward(0)
    after(14)
    after(15)
    project_qkv(2)
    weights_last(0)
    weights_cross(2)
    for i in (6, 7, 10, 11, 16, 17):
        after(i)
    project_qkv(3)

    s_copies = [
        remote(sums.at[t], sums.at[t], s_send.at[n], s_recv.at[n], {"tensor": lax.rem(t + n, 8)}) for n in range(1, 8)
    ]
    for c in gc:
        c.wait_send()
    for c in s_copies:
        c.start()
    weights_turn(1)
    for n in range(1, 8):
        there = sums.at[lax.rem(t + 8 - n, 8)]
        remote(there, there, s_send.at[n], s_recv.at[n], {"tensor": lax.rem(t + n, 8)}).wait_recv()
    for slot in range(8):
        total = sums[0, chunk_of[slot]]
        for other in range(1, 8):
            total = total + sums[other, chunk_of[slot]]
        scale = lax.rsqrt(total / (HEADS * HD) + EPS)
        rows = pl.ds(slot * CH, CH)
        for j, (out, g, extra) in enumerate(((q, q_gain, HD**-0.5), (k, k_gain, 1.0))):
            col = jnp.transpose(jnp.broadcast_to(scale[:, j * HD : (j + 1) * HD], (CH, HD))) * extra
            gains = g[...].reshape(1, LW)
            for h in range(LH):
                lanes = slice(h * HD, (h + 1) * HD)
                out[h, rows] = (qk[j, rows, lanes] * col * gains[:, lanes]).astype(BF16)

    def attend(first, second, dst, place):
        def one(h, _):
            for n, slot in enumerate((first, second)):
                rows = pl.ds(slot * CH, CH)
                scores = lax.dot_general(q[h, rows], k[h], (((1,), (1,)), ((), ())), preferred_element_type=F32)
                e = jnp.exp(scores - jnp.max(scores, axis=-1, keepdims=True))
                total = jnp.sum(e, axis=-1, keepdims=True)
                part = jnp.dot(e.astype(BF16), v[h], preferred_element_type=F32)
                dst[place + n, :, pl.ds(pl.multiple_of(h * HD, HD), HD)] = (part / total).astype(BF16)
            return _

        lax.fori_loop(0, LH, one, 0)

    mc = [remote(far.at[n], mix.at[1, n], m_send.at[n], m_recv.at[n], directions()["x"]) for n in range(4)]
    rc = [
        remote(ob.at[src, pl.ds(row, 32)], xg.at[4 + i // 4, pl.ds(32 * (i % 4), 32)], r_send.at[i], r_recv.at[i], directions()[way])
        for i, (src, row, way, _) in enumerate(SCATTER)
    ]
    ec = table_copies(SPREAD, xg, e_send, e_recv)

    def branch(n):
        for i in (n, n + 1):
            mc[i].wait_recv()
        mine = mix[0, n : n + 2].reshape(2 * CH, LW)
        other = mix[1, n : n + 2].reshape(2 * CH, LW)
        for n0 in range(0, D, 640):
            cols = slice(n0, n0 + 640)
            part = jnp.dot(mine, wo[0, :, cols], preferred_element_type=F32)
            part = (part + jnp.dot(other, wo[1, :, cols], preferred_element_type=F32)).astype(BF16)
            ob[n, :, cols] = part[:CH]
            ob[n + 1, :, cols] = part[CH:]

    def add(i):
        rc[i].wait_recv()
        _, row, _, dst = SCATTER[i]
        total = ob[dst, row : row + 32].astype(F32) + xg[4 + i // 4, 32 * (i % 4) : 32 * (i % 4) + 32].astype(F32)
        ob[dst, row : row + 32] = total.astype(BF16)

    attend(X2, X1, far, 0)
    mc[0].start()
    mc[1].start()
    weights_cross(3)
    attend(O2, O1, mix.at[0], 0)
    own_copies[0].wait()
    weights_here(0)
    branch(0)
    for i in (0, 1, 6, 7, 2, 8):
        rc[i].start()
    weights_turn(2)
    weights_forward(1)
    attend(XM, X0, far, 2)
    mc[2].start()
    mc[3].start()
    weights_cross(4)
    attend(OM, O0, mix.at[0], 2)
    branch(2)
    for i in (4, 10):
        rc[i].start()
    for b in (0, 6):
        add(b)
        rc[b + 3].start()
        add(b + 1)
        rc[b + 5].start()
    weights_last(1)
    weights_turn(3)
    weights_forward(2)

    def encode(row0):
        base = jnp.dot(merge_order(row0, 32), patches[...], preferred_element_type=F32)
        total = ob[N0, row0 : row0 + 32].astype(F32)
        xg[N0, pl.ds(row0, 32)] = (base + layer_scale[...].reshape(1, D) * total).astype(BF16)

    def encode_half(half):
        for i in (2, 4, 3, 5):
            add(6 * half + i)
        encode(64 * half)
        encode(64 * half + 32)
        ec[4 * half].start()
        ec[4 * half + 1].start()

    encode_half(0)
    weights_last(2)
    weights_turn(4)
    weights_forward(3)
    encode_half(1)
    for c in rc + mc:
        c.wait_send()

    def forward(half):
        ec[4 * half].wait_recv()
        ec[4 * half + 2].start()
        ec[4 * half + 1].wait_recv()
        ec[4 * half + 3].start()

    def project(ab, total):
        weights_here(1 + ab)
        x = xg[0:4, ab * 32 : (ab + 1) * 32, :].reshape(4 * 32, D)
        rows = slice(ab * D, (ab + 1) * D)
        return [sofar + jnp.dot(x, wp[c, rows, :], preferred_element_type=F32) for c, sofar in enumerate(total)]

    forward(0)
    weights_last(3)
    weights_forward(4)
    forward(1)
    own_copies[1].wait()
    ec[2].wait_recv()
    ec[3].wait_recv()
    total = project(0, [jnp.zeros((CH, 512), F32)] * 2)
    weights_last(4)
    total = project(1, total)
    ec[6].wait_recv()
    ec[7].wait_recv()
    total = project(2, total)
    total = project(3, total)
    for c in range(2):
        out = total[c].astype(BF16)
        for n, slot in ((N2, O2), (N1, O1), (NM, OM), (N0, O0)):
            place = 2 * lax.rem(chunk_of[slot], 4)
            proj[c, pl.ds(place, 2)] = out[n * 32 : (n + 1) * 32].reshape(2, 16, 512)
    for c in ec + [c for copies in wc for c in copies]:
        c.wait_send()

    mine = me // 8 == xh

    def piece_copy(n, c):
        m = lax.rem(me + n, 8)
        target = group(8 * xh + m, (t, opp)[c])
        return remote(proj.at[c, m], pieces.at[me], a_send.at[c, n], a_recv.at[me], target)

    def first_copies(act):
        for n in range(1, 8):
            for c in range(2):
                act(piece_copy(n, c))
        act(piece_copy(0, 1))

        @pl.when(jnp.logical_not(mine))
        def _():
            act(piece_copy(0, 0))

    first_copies(lambda c: c.start())

    @pl.when(mine)
    def _():
        pieces[me] = proj[0, lax.rem(me, 8)]

    def piece_here(g):
        remote(pieces.at[g], pieces.at[g], a_send.at[0, 0], a_recv.at[g], group(me, opp)).wait_recv()

    for n in range(1, 16):
        piece_here(lax.rem(me + n, 16))

    @pl.when(jnp.logical_not(mine))
    def _():
        piece_here(me)

    start = jnp.int32(0)
    for g in range(16):
        for s in range(2):
            tile = slots[jnp.minimum(start + s, 15)]
            picked[g, s] = pieces[tile]
        start = start + counts[g]
    second = [
        remote(
            picked.at[lax.rem(me + n, 16)], arrive.at[me], b_send.at[n], b_recv.at[n], group(lax.rem(me + n, 16), t)
        )
        for n in range(1, 16)
    ]
    for c in second:
        c.start()
    arrive[me] = picked[me]
    for n in range(1, 16):
        there = arrive.at[lax.rem(me + 16 - n, 16)]
        remote(there, there, b_send.at[n], b_recv.at[n], group(lax.rem(me + n, 16), t)).wait_recv()
    for n in range(16):
        for s in range(2):
            feats[s * 256 + n * 16 : s * 256 + n * 16 + 16, :] = arrive[n, s]
    first_copies(lambda c: c.wait_send())
    for c in s_copies + second:
        c.wait_send()


def place_kernel(feats, text, counts, offsets, out):
    me = lax.axis_index("section") * 2 + lax.axis_index("dp")
    rows = counts[me] * 256
    offset = offsets[me]
    seq = text.shape[0]
    for r0 in range(0, seq, 256):
        r = lax.broadcasted_iota(jnp.int32, (256, 512), 0) + r0 - offset
        c = lax.broadcasted_iota(jnp.int32, (256, 512), 1)
        pick = (r == c).astype(F32).astype(BF16)
        moved = jnp.dot(pick, feats[...], preferred_element_type=F32)
        inside = (r >= 0) & (r < rows)
        out[r0 : r0 + 256, :] = jnp.where(inside, moved, text[r0 : r0 + 256, :].astype(F32)).astype(BF16)


def spec(space):
    return pl.BlockSpec(memory_space=space)


def shards(
    patches,
    norm_gain,
    w_qkv,
    q_gain,
    k_gain,
    w_out,
    layer_scale,
    w_proj,
    text_embed,
    tile_counts,
    image_offsets,
    tile_slots,
):
    dma = pltpu.SemaphoreType.DMA
    smem = pltpu.SMEM
    heads = VMEM((LH, 8 * CH, HD), BF16)
    feats = pl.pallas_call(
        encode_kernel,
        out_shape=jax.ShapeDtypeStruct((512, 512), BF16),
        in_specs=[spec(s) for s in (VMEM, VMEM, pl.ANY, VMEM, VMEM, VMEM, pl.ANY, pl.ANY, smem, smem)],
        out_specs=spec(VMEM),
        scratch_shapes=[
            VMEM((8, CH, D), BF16),
            VMEM((3, D, LW), BF16),
            VMEM((2, 8 * CH, LW), F32),
            VMEM((8, 8, 1, 2 * HD), F32),
            heads,
            heads,
            heads,
            VMEM((2, LW, D), BF16),
            VMEM((2, 4 * D, 512), BF16),
            VMEM((2, 4, CH, LW), BF16),
            VMEM((4, CH, LW), BF16),
            VMEM((4, CH, D), BF16),
            VMEM((2, 8, 16, 512), BF16),
            VMEM((16, 16, 512), BF16),
            VMEM((16, 2, 16, 512), BF16),
            VMEM((16, 2, 16, 512), BF16),
            dma((5,)),
            dma((len(GATHER),)),
            dma((len(GATHER),)),
            dma((8,)),
            dma((8,)),
            dma((len(SETS), 10)),
            dma((len(SETS), 10)),
            dma((4,)),
            dma((4,)),
            dma((len(SCATTER),)),
            dma((len(SCATTER),)),
            dma((len(SPREAD),)),
            dma((len(SPREAD),)),
            dma((2, 8)),
            dma((16,)),
            dma((16,)),
            dma((16,)),
        ],
        compiler_params=pltpu.CompilerParams(collective_id=0, **PARAMS),
        name="encode",
    )(
        patches[0],
        norm_gain,
        w_qkv.transpose(1, 0, 2),
        q_gain,
        k_gain,
        layer_scale,
        w_out,
        w_proj,
        tile_counts,
        tile_slots,
    )
    out = pl.pallas_call(
        place_kernel,
        out_shape=jax.ShapeDtypeStruct(text_embed.shape[1:], BF16),
        in_specs=[spec(VMEM)] * 2 + [spec(smem)] * 2,
        out_specs=spec(VMEM),
        compiler_params=pltpu.CompilerParams(vmem_limit_bytes=32 * 1024 * 1024),
        name="place",
    )(feats, text_embed[0], tile_counts, image_offsets)
    return out[None]


def solution(mesh):
    placed = (
        P(("section", "dp"), "tensor", None),
        P(),
        P(None, None, "tensor"),
        P("tensor"),
        P("tensor"),
        P("tensor", None),
        P(),
        P(None, "tensor"),
        P(("section", "dp"), None, "tensor"),
        P(),
        P(),
        P(),
    )
    return jax.shard_map(
        shards,
        mesh=mesh,
        in_specs=placed,
        out_specs=P(("section", "dp"), None, "tensor"),
        check_vma=False,
    )
```

time: 451 us -> 157 us (0.35)
  waiting for transfers between devices: 315 us -> 0 us
  Pallas kernels: 0 us -> 156 us
  matrix products: 48.5 us -> 0 us
  local copies, waits for them, and re-layouts: 38.6 us -> 1.05 us
  blocking collectives: 16.8 us -> 0 us
  between operations: 16.3 us -> 0.05 us
  other arithmetic: 14.7 us -> 0 us
    all_gather x3 -> x0, waiting for transfers between devices: 212 us -> none  [the longest x1 89.3 us: shards(): shard_rows = lax.all_gather(merged, 'tensor', axis=1, tiled=True)]
    pallas_call x0 -> x2, Pallas kernels: none -> 156 us  [the longest x1 154 us: shards(): pl.pallas_call(encode_kernel, out_shape=jax.ShapeDtypeStruct((512, 512),...]
    reduce_scatter x1 -> x0, waiting for transfers between devices: 103 us -> none  [shards(): lax.psum_scatter(flat.reshape(rows_here * lax.axis_size('tensor'), tiles_...]
    dot_general x5 -> x0, matrix products: 38.4 us -> none  [the longest x1 13.3 us: shards(): jnp.dot(shard_rows.reshape(-1, width_d), w_flat, preferred_element_type=j...]
    psum x1 -> x0, blocking collectives: 16.8 us -> none  [shards(): lax.psum((jnp.sum(query_part * query_part, axis=-1), jnp.sum(key_part * k...]
    reshape x5 -> x0, local copies, waits for them, and re-layouts: 13 us -> none  [the longest x1 4.84 us: shards(): shard_tiles.reshape(count_tiles, -1)]
    unnamed x21 -> x8, local copies, waits for them, and re-layouts: 13.2 us -> 1.05 us
    sub x1 -> x0, matrix products: 10.1 us -> none  [shards(): weights = jax.nn.softmax(scores, axis=-1).astype(jnp.bfloat16)]
  transfers between devices with their start and end apart: 4 -> 0, of which waited for: 4 -> 0; matrix products, arithmetic and copies ran while one was open for 4% -> 0% of each run, Pallas kernels for 0% -> 0%
where the time goes in v2:
time: 157 us
  Pallas kernels  156 us (99%)
    pallas_call x1, Pallas kernels, shards(): pl.pallas_call(encode_kernel, out_shape=jax.ShapeDtypeStruct((512, 512),...  154 us

profile of v2, /device:TPU:1, one launch (start us, length us, event | category | flops | bytes accessed | tf_op | source)
XLA Modules:
  0.0 157.2 jit_solution(15140427612403540648)
XLA Ops:
  0.0 0.0 copy-start.1
  0.0 0.0 copy-start.2
  0.0 0.0 copy-start.3
  0.0 154.1 %encode.1.feats = bf16[512,512]{1,0:T(8,128)(2,1)} custom-call(bf16[128,3200]{1,0:T(8,128)(2,1)} %bitcast.6, f32[3200]{0:T(1024)} %gain.1, bf16[3,3200,384]{2,1,0:T(8,128)(2,1)} %bitcast.5, f32[384]{0:T(512)} %q_gain.1, f32[384]{0:T(512)} %k_gain.1, f32[3200]{0:T(1024)} %layer_scale.1, bf16[384,3200]{1,0:T(8,128)(2,1)} %wo_hbm.1, bf16[12800,512]{1,0:T(8,128)(2,1)} %wp_hbm.1, ...), custom_call_target="tpu_custom_call" | custom-call | tf_op jit(solution)/shard_map/encode/pallas_call | solution.py:495
  154.1 0.0 copy-done.1
  154.1 0.0 copy-done.2
  154.1 0.0 copy-done.3
  154.1 0.0 copy-start
  154.1 1.0 copy-done
  155.2 2.0 %place.1 = bf16[768,512]{1,0:T(8,128)(2,1)} custom-call(bf16[512,512]{1,0:T(8,128)(2,1)S(1)} %copy-done, bf16[768,512]{1,0:T(8,128)(2,1)S(1)} %bitcast.4, s32[16]{0:T(128)S(1)} %copy-done.2, s32[16]{0:T(128)S(1)} %copy-done.3), custom_call_target="tpu_custom_call" | custom-call | tf_op jit(solution)/shard_map/place/pallas_call | solution.py:549
Async XLA Ops:
  0.0 154.1 %copy-start.1 = (bf16[1,768,512]{2,1,0:T(8,128)(2,1)S(1)}, bf16[1,768,512]{2,1,0:T(8,128)(2,1)}, u32[]{:S(2)}) copy-start(bf16[1,768,512]{2,1,0:T(8,128)(2,1)} %param.20) | copy-start | bytes 2359300
  0.0 154.1 %copy-start.2 = (s32[16]{0:T(128)S(1)}, s32[16]{0:T(128)}, u32[]{:S(2)}) copy-start(s32[16]{0:T(128)} %counts.3) | copy-start | bytes 196
  0.0 154.1 %copy-start.3 = (s32[16]{0:T(128)S(1)}, s32[16]{0:T(128)}, u32[]{:S(2)}) copy-start(s32[16]{0:T(128)} %offsets.1) | copy-start | bytes 196
  154.1 1.0 copy-start

commit v3 on v2

--- a/solution.py
+++ b/solution.py
@@ -15,6 +15,7 @@
 BF16 = jnp.bfloat16
 MESH = pl.DeviceIdType.MESH
 EPS = 1e-06
+LOG2E = 1.4426950408889634
 VMEM = pltpu.VMEM
 PARAMS = dict(has_side_effects=True, vmem_limit_bytes=62 * 1024 * 1024)
 
@@ -22,24 +23,24 @@
 N2, N1, NM, N0 = range(4)
 
 GATHER = (
-    (O0, 0, 80, "x", X0),
-    (O0, 0, 80, "p", OM),
-    (O0, 0, 80, "m", O1),
-    (O0, 80, 48, "p", OM),
-    (O0, 80, 48, "m", O1),
-    (O0, 80, 48, "x", X0),
+    (O0, 0, 96, "x", X0),
+    (O0, 0, 96, "p", OM),
+    (O0, 0, 96, "m", O1),
+    (O0, 96, 32, "p", OM),
+    (O0, 96, 32, "m", O1),
+    (O0, 96, 32, "x", X0),
     (OM, 0, 48, "p", O2),
-    (O1, 48, 32, "m", O2),
-    (X0, 0, 80, "p", XM),
-    (X0, 0, 80, "m", X1),
+    (O1, 48, 48, "m", O2),
+    (X0, 0, 96, "p", XM),
+    (X0, 0, 96, "m", X1),
     (XM, 0, 48, "p", X2),
-    (X1, 48, 32, "m", X2),
-    (OM, 80, 16, "p", O2),
-    (O1, 96, 32, "m", O2),
-    (OM, 80, 48, "x", XM),
-    (O1, 80, 48, "x", X1),
-    (O2, 80, 16, "x", X2),
-    (O2, 96, 32, "x", X2),
+    (X1, 48, 48, "m", X2),
+    (OM, 96, 16, "p", O2),
+    (O1, 112, 16, "m", O2),
+    (OM, 96, 32, "x", XM),
+    (O1, 96, 32, "x", X1),
+    (O2, 96, 16, "x", X2),
+    (O2, 112, 16, "x", X2),
 )
 
 SCATTER = tuple(
@@ -105,17 +106,17 @@
     ]
 
 
-def weight_copies(number, source, buf, base, send, recv):
+def weight_copies(number, source, buf, base, send, recv, source_base=0):
     rows, first = SETS[number]
     section = lax.axis_index("section")
     where = directions()
 
-    def part(ref, offset, which):
+    def part(ref, offset, which, base=base):
         start = base + lax.rem(section + 8 + offset, 8) * rows
         start, count = ((start, rows), (start, first), (start + first, rows - first))[which]
         return ref.at[pl.ds(pl.multiple_of(start, 16), count)]
 
-    copies = [remote(part(source, 0, 0), part(buf, 0, 0), send.at[number, 0], recv.at[number, 0], where["cross"])]
+    copies = [remote(part(source, 0, 0, source_base), part(buf, 0, 0), send.at[number, 0], recv.at[number, 0], where["cross"])]
     for i, (offset, which, way) in enumerate(WEIGHTS):
         there = part(buf, offset, which)
         copies.append(remote(there, there, send.at[number, i + 1], recv.at[number, i + 1], where[way]))
@@ -145,7 +146,7 @@
 
     w_copies = [pltpu.make_async_copy(w_hbm.at[j], w.at[j], w_sem.at[j]) for j in range(3)]
     own_copies = [
-        pltpu.make_async_copy(wo_hbm, wo.at[0], w_sem.at[3]),
+        pltpu.make_async_copy(wo_hbm, wo.at[pl.ds(0, LW)], w_sem.at[3]),
         pltpu.make_async_copy(wp_hbm, wp.at[0], w_sem.at[4]),
     ]
     for c in w_copies + own_copies:
@@ -153,10 +154,8 @@
     barrier = pltpu.get_barrier_semaphore()
     for n in range(1, 8):
         pl.semaphore_signal(barrier, inc=1, device_id={"tensor": lax.rem(t + n, 8)}, device_id_type=MESH)
-    for n in range(1, 16):
-        for tensor in (t, opp):
-            target = group(lax.rem(me + n, 16), tensor)
-            pl.semaphore_signal(barrier, inc=1, device_id=target, device_id_type=MESH)
+    for way in ("cross", "u", "d", "c"):
+        pl.semaphore_signal(barrier, inc=1, device_id=directions()[way], device_id_type=MESH)
 
     def norm(row0, rows):
         x = jnp.dot(merge_order(row0, rows), patches[...], preferred_element_type=F32)
@@ -164,8 +163,8 @@
         xg[O0, pl.ds(row0, rows)] = (x * scale * gain[...].reshape(1, D)).astype(BF16)
 
     gc = table_copies(GATHER, xg, g_send, g_recv)
-    wc = [weight_copies(0, wo_hbm, wo.at[1], 0, x_send, x_recv)]
-    wc += [weight_copies(1 + ab, wp_hbm, wp.at[1], ab * D, x_send, x_recv) for ab in range(4)]
+    wc = [weight_copies(0, wo_hbm, wo, LW, x_send, x_recv)]
+    wc += [weight_copies(1 + ab, wp_hbm, wp.at[1], ab * D, x_send, x_recv, ab * D) for ab in range(4)]
 
     def weights_cross(n):
         wc[n][0].start()
@@ -195,12 +194,11 @@
 
     norm(0, 32)
     norm(32, 32)
-    norm(64, 16)
-    pl.semaphore_wait(barrier, 37)
+    norm(64, 32)
+    pl.semaphore_wait(barrier, 11)
     for i in (0, 1, 2):
         gc[i].start()
     weights_cross(0)
-    norm(80, 16)
     norm(96, 32)
     for i in (3, 4, 5):
         gc[i].start()
@@ -212,7 +210,7 @@
         for i in then:
             gc[i].start()
 
-    def project_qkv(g):
+    def project_qk(g):
         x = xg[2 * g : 2 * g + 2].reshape(2 * CH, D)
         rows = pl.ds(2 * g * CH, 2 * CH)
         for j in range(2):
@@ -224,9 +222,12 @@
                 sq = sq[:, :HD] + sq[:, HD : 2 * HD] + sq[:, 2 * HD :]
                 row = jnp.sum(jnp.transpose(sq), axis=0, keepdims=True)
                 sums[t, chunk_of[2 * g + u], :, j * HD : (j + 1) * HD] = row
+
+    def project_v(g):
+        x = xg[2 * g : 2 * g + 2].reshape(2 * CH, D)
         part = jnp.dot(x, w[2], preferred_element_type=F32).astype(BF16)
         for h in range(LH):
-            v[h, rows] = part[:, h * HD : (h + 1) * HD]
+            v[h, pl.ds(2 * g * CH, 2 * CH), :HD] = part[:, h * HD : (h + 1) * HD]
 
     after(1, 6)
     after(2, 7)
@@ -234,23 +235,27 @@
     after(3, 12, 14)
     after(4, 13, 15)
     after(5)
-    project_qkv(0)
+    project_qk(0)
+    project_v(0)
     after(8, 10)
     after(9, 11)
     after(12, 16)
     after(13, 17)
     weights_turn(0)
     weights_cross(1)
-    project_qkv(1)
+    project_qk(1)
+    project_v(1)
+    v[:, :, HD:] = jnp.ones((LH, 8 * CH, HD), BF16)
     weights_forward(0)
     after(14)
     after(15)
-    project_qkv(2)
+    project_qk(2)
+    project_v(2)
     weights_last(0)
+    for i in (6, 7, 16, 17, 10, 11):
+        after(i)
     weights_cross(2)
-    for i in (6, 7, 10, 11, 16, 17):
-        after(i)
-    project_qkv(3)
+    project_qk(3)
 
     s_copies = [
         remote(sums.at[t], sums.at[t], s_send.at[n], s_recv.at[n], {"tensor": lax.rem(t + n, 8)}) for n in range(1, 8)
@@ -259,6 +264,7 @@
         c.wait_send()
     for c in s_copies:
         c.start()
+    project_v(3)
     weights_turn(1)
     for n in range(1, 8):
         there = sums.at[lax.rem(t + 8 - n, 8)]
@@ -269,22 +275,23 @@
             total = total + sums[other, chunk_of[slot]]
         scale = lax.rsqrt(total / (HEADS * HD) + EPS)
         rows = pl.ds(slot * CH, CH)
-        for j, (out, g, extra) in enumerate(((q, q_gain, HD**-0.5), (k, k_gain, 1.0))):
+        for j, (out, g, extra) in enumerate(((q, q_gain, HD**-0.5 * LOG2E), (k, k_gain, 1.0))):
             col = jnp.transpose(jnp.broadcast_to(scale[:, j * HD : (j + 1) * HD], (CH, HD))) * extra
             gains = g[...].reshape(1, LW)
             for h in range(LH):
                 lanes = slice(h * HD, (h + 1) * HD)
                 out[h, rows] = (qk[j, rows, lanes] * col * gains[:, lanes]).astype(BF16)
 
-    def attend(first, second, dst, place):
+    def attend(slot, *places):
         def one(h, _):
-            for n, slot in enumerate((first, second)):
-                rows = pl.ds(slot * CH, CH)
-                scores = lax.dot_general(q[h, rows], k[h], (((1,), (1,)), ((), ())), preferred_element_type=F32)
-                e = jnp.exp(scores - jnp.max(scores, axis=-1, keepdims=True))
-                total = jnp.sum(e, axis=-1, keepdims=True)
-                part = jnp.dot(e.astype(BF16), v[h], preferred_element_type=F32)
-                dst[place + n, :, pl.ds(pl.multiple_of(h * HD, HD), HD)] = (part / total).astype(BF16)
+            rows = pl.ds(slot * CH, 2 * CH)
+            scores = lax.dot_general(q[h, rows], k[h], (((1,), (1,)), ((), ())), preferred_element_type=F32)
+            e = jnp.exp2(scores - jnp.max(scores, axis=-1, keepdims=True)).astype(BF16)
+            part = jnp.dot(e, v[h], preferred_element_type=F32)
+            part = (part[:, :HD] / part[:, HD:]).astype(BF16)
+            lanes = pl.ds(pl.multiple_of(h * HD, HD), HD)
+            for n, (dst, place) in enumerate(places):
+                dst[place, :, lanes] = part[n * CH : (n + 1) * CH]
             return _
 
         lax.fori_loop(0, LH, one, 0)
@@ -296,17 +303,15 @@
     ]
     ec = table_copies(SPREAD, xg, e_send, e_recv)
 
-    def branch(n):
-        for i in (n, n + 1):
+    def branch(n, count):
+        for i in range(n, n + count):
             mc[i].wait_recv()
-        mine = mix[0, n : n + 2].reshape(2 * CH, LW)
-        other = mix[1, n : n + 2].reshape(2 * CH, LW)
-        for n0 in range(0, D, 640):
-            cols = slice(n0, n0 + 640)
-            part = jnp.dot(mine, wo[0, :, cols], preferred_element_type=F32)
-            part = (part + jnp.dot(other, wo[1, :, cols], preferred_element_type=F32)).astype(BF16)
-            ob[n, :, cols] = part[:CH]
-            ob[n + 1, :, cols] = part[CH:]
+        x = jnp.concatenate([mix[c, n : n + count].reshape(count * CH, LW) for c in range(2)], axis=1)
+        for n0 in range(0, D, 1280):
+            cols = slice(n0, min(n0 + 1280, D))
+            part = jnp.dot(x, wo[:, cols], preferred_element_type=F32).astype(BF16)
+            for i in range(count):
+                ob[n + i, :, cols] = part[i * CH : (i + 1) * CH]
 
     def add(i):
         rc[i].wait_recv()
@@ -314,34 +319,39 @@
         total = ob[dst, row : row + 32].astype(F32) + xg[4 + i // 4, 32 * (i % 4) : 32 * (i % 4) + 32].astype(F32)
         ob[dst, row : row + 32] = total.astype(BF16)
 
-    attend(X2, X1, far, 0)
-    mc[0].start()
-    mc[1].start()
-    weights_cross(3)
-    attend(O2, O1, mix.at[0], 0)
+    own, off = mix.at[0], far
+    attend(O2, (own, N2), (off, N2))
+    mc[N2].start()
+    attend(X1, (off, N1), (off, NM))
+    mc[N1].start()
+    mc[NM].start()
     own_copies[0].wait()
     weights_here(0)
-    branch(0)
-    for i in (0, 1, 6, 7, 2, 8):
+    branch(N2, 1)
+    for i in (0, 1, 6, 7):
+        rc[i].start()
+    attend(O1, (own, N1), (own, NM))
+    branch(N1, 2)
+    for i in (2, 4):
         rc[i].start()
     weights_turn(2)
+    weights_cross(3)
+    attend(O0, (own, N0), (off, N0))
+    mc[N0].start()
+    add(0)
+    rc[3].start()
+    add(1)
+    rc[5].start()
+    for i in (8, 10):
+        rc[i].start()
     weights_forward(1)
-    attend(XM, X0, far, 2)
-    mc[2].start()
-    mc[3].start()
+    branch(N0, 1)
     weights_cross(4)
-    attend(OM, O0, mix.at[0], 2)
-    branch(2)
-    for i in (4, 10):
-        rc[i].start()
-    for b in (0, 6):
-        add(b)
-        rc[b + 3].start()
-        add(b + 1)
-        rc[b + 5].start()
-    weights_last(1)
+    add(6)
+    rc[9].start()
+    add(7)
+    rc[11].start()
     weights_turn(3)
-    weights_forward(2)
 
     def encode(row0):
         base = jnp.dot(merge_order(row0, 32), patches[...], preferred_element_type=F32)
@@ -357,10 +367,12 @@
         ec[4 * half + 1].start()
 
     encode_half(0)
+    weights_last(1)
+    weights_forward(2)
+    weights_turn(4)
+    encode_half(1)
+    weights_forward(3)
     weights_last(2)
-    weights_turn(4)
-    weights_forward(3)
-    encode_half(1)
     for c in rc + mc:
         c.wait_send()
 
@@ -377,15 +389,15 @@
         return [sofar + jnp.dot(x, wp[c, rows, :], preferred_element_type=F32) for c, sofar in enumerate(total)]
 
     forward(0)
+    weights_forward(4)
     weights_last(3)
-    weights_forward(4)
     forward(1)
     own_copies[1].wait()
     ec[2].wait_recv()
     ec[3].wait_recv()
     total = project(0, [jnp.zeros((CH, 512), F32)] * 2)
+    total = project(1, total)
     weights_last(4)
-    total = project(1, total)
     ec[6].wait_recv()
     ec[7].wait_recv()
     total = project(2, total)
@@ -492,6 +504,7 @@
     dma = pltpu.SemaphoreType.DMA
     smem = pltpu.SMEM
     heads = VMEM((LH, 8 * CH, HD), BF16)
+    values = VMEM((LH, 8 * CH, 2 * HD), BF16)
     feats = pl.pallas_call(
         encode_kernel,
         out_shape=jax.ShapeDtypeStruct((512, 512), BF16),
@@ -504,8 +517,8 @@
             VMEM((8, 8, 1, 2 * HD), F32),
             heads,
             heads,
-            heads,
-            VMEM((2, LW, D), BF16),
+            values,
+            VMEM((2 * LW, D), BF16),
             VMEM((2, 4 * D, 512), BF16),
             VMEM((2, 4, CH, LW), BF16),
             VMEM((4, CH, LW), BF16),

time: 157 us -> 154 us (0.981)
  Pallas kernels: 156 us -> 153 us
    pallas_call x1, Pallas kernels: 154 us -> 151 us  [shards(): pl.pallas_call(encode_kernel, out_shape=jax.ShapeDtypeStruct((512, 512),...]
where the time goes in v3:
time: 154 us
  Pallas kernels  153 us (99%)
    pallas_call x1, Pallas kernels, shards(): pl.pallas_call(encode_kernel, out_shape=jax.ShapeDtypeStruct((512, 512),...  151 us

profile of v3, /device:TPU:1, one launch (start us, length us, event | category | flops | bytes accessed | tf_op | source)
XLA Modules:
  0.0 154.0 jit_solution(7859774252167862760)
XLA Ops:
  0.0 0.0 copy-start.1
  0.0 0.0 copy-start.2
  0.0 0.0 copy-start.3
  0.0 150.9 %encode.1.feats = bf16[512,512]{1,0:T(8,128)(2,1)} custom-call(bf16[128,3200]{1,0:T(8,128)(2,1)} %bitcast.6, f32[3200]{0:T(1024)} %gain.1, bf16[3,3200,384]{2,1,0:T(8,128)(2,1)} %bitcast.5, f32[384]{0:T(512)} %q_gain.1, f32[384]{0:T(512)} %k_gain.1, f32[3200]{0:T(1024)} %layer_scale.1, bf16[384,3200]{1,0:T(8,128)(2,1)} %wo_hbm.1, bf16[12800,512]{1,0:T(8,128)(2,1)} %wp_hbm.1, ...), custom_call_target="tpu_custom_call" | custom-call | tf_op jit(solution)/shard_map/encode/pallas_call | solution.py:508
  150.9 0.0 copy-done.1
  150.9 0.0 copy-done.2
  150.9 0.0 copy-done.3
  150.9 0.0 copy-start
  150.9 1.0 copy-done
  152.0 2.0 %place.1 = bf16[768,512]{1,0:T(8,128)(2,1)} custom-call(bf16[512,512]{1,0:T(8,128)(2,1)S(1)} %copy-done, bf16[768,512]{1,0:T(8,128)(2,1)S(1)} %bitcast.4, s32[16]{0:T(128)S(1)} %copy-done.2, s32[16]{0:T(128)S(1)} %copy-done.3), custom_call_target="tpu_custom_call" | custom-call | tf_op jit(solution)/shard_map/place/pallas_call | solution.py:562
Async XLA Ops:
  0.0 150.9 %copy-start.1 = (bf16[1,768,512]{2,1,0:T(8,128)(2,1)S(1)}, bf16[1,768,512]{2,1,0:T(8,128)(2,1)}, u32[]{:S(2)}) copy-start(bf16[1,768,512]{2,1,0:T(8,128)(2,1)} %param.20) | copy-start | bytes 2359300
  0.0 150.9 %copy-start.2 = (s32[16]{0:T(128)S(1)}, s32[16]{0:T(128)}, u32[]{:S(2)}) copy-start(s32[16]{0:T(128)} %counts.3) | copy-start | bytes 196
  0.0 150.9 %copy-start.3 = (s32[16]{0:T(128)S(1)}, s32[16]{0:T(128)}, u32[]{:S(2)}) copy-start(s32[16]{0:T(128)} %offsets.1) | copy-start | bytes 196
  150.9 1.0 copy-start

commit v4 on v3

--- a/solution.py
+++ b/solution.py
@@ -196,9 +196,9 @@
     norm(32, 32)
     norm(64, 32)
     pl.semaphore_wait(barrier, 11)
+    weights_cross(0)
     for i in (0, 1, 2):
         gc[i].start()
-    weights_cross(0)
     norm(96, 32)
     for i in (3, 4, 5):
         gc[i].start()
@@ -237,11 +237,11 @@
     after(5)
     project_qk(0)
     project_v(0)
+    weights_turn(0)
     after(8, 10)
     after(9, 11)
     after(12, 16)
     after(13, 17)
-    weights_turn(0)
     weights_cross(1)
     project_qk(1)
     project_v(1)
@@ -269,20 +269,25 @@
     for n in range(1, 8):
         there = sums.at[lax.rem(t + 8 - n, 8)]
         remote(there, there, s_send.at[n], s_recv.at[n], {"tensor": lax.rem(t + n, 8)}).wait_recv()
+    def scale(slot, j):
+        total = sums[0, chunk_of[slot], :, j * HD : (j + 1) * HD]
+        for other in range(1, 8):
+            total = total + sums[other, chunk_of[slot], :, j * HD : (j + 1) * HD]
+        factor = lax.rsqrt(total / (HEADS * HD) + EPS)
+        out, gains, extra = ((q, q_gain, HD**-0.5 * LOG2E), (k, k_gain, 1.0))[j]
+        col = jnp.transpose(jnp.broadcast_to(factor, (CH, HD))) * extra
+        gains = gains[...].reshape(1, LW)
+        for h in range(LH):
+            lanes = slice(h * HD, (h + 1) * HD)
+            out[h, pl.ds(slot * CH, CH)] = (qk[j, pl.ds(slot * CH, CH), lanes] * col * gains[:, lanes]).astype(BF16)
+
     for slot in range(8):
-        total = sums[0, chunk_of[slot]]
-        for other in range(1, 8):
-            total = total + sums[other, chunk_of[slot]]
-        scale = lax.rsqrt(total / (HEADS * HD) + EPS)
-        rows = pl.ds(slot * CH, CH)
-        for j, (out, g, extra) in enumerate(((q, q_gain, HD**-0.5 * LOG2E), (k, k_gain, 1.0))):
-            col = jnp.transpose(jnp.broadcast_to(scale[:, j * HD : (j + 1) * HD], (CH, HD))) * extra
-            gains = g[...].reshape(1, LW)
-            for h in range(LH):
-                lanes = slice(h * HD, (h + 1) * HD)
-                out[h, rows] = (qk[j, rows, lanes] * col * gains[:, lanes]).astype(BF16)
+        scale(slot, 1)
 
     def attend(slot, *places):
+        scale(slot, 0)
+        scale(slot + 1, 0)
+
         def one(h, _):
             rows = pl.ds(slot * CH, 2 * CH)
             scores = lax.dot_general(q[h, rows], k[h], (((1,), (1,)), ((), ())), preferred_element_type=F32)
@@ -382,11 +387,9 @@
         ec[4 * half + 1].wait_recv()
         ec[4 * half + 3].start()
 
-    def project(ab, total):
-        weights_here(1 + ab)
+    def project(ab, c):
         x = xg[0:4, ab * 32 : (ab + 1) * 32, :].reshape(4 * 32, D)
-        rows = slice(ab * D, (ab + 1) * D)
-        return [sofar + jnp.dot(x, wp[c, rows, :], preferred_element_type=F32) for c, sofar in enumerate(total)]
+        return jnp.dot(x, wp[c, ab * D : (ab + 1) * D, :], preferred_element_type=F32)
 
     forward(0)
     weights_forward(4)
@@ -395,20 +398,14 @@
     own_copies[1].wait()
     ec[2].wait_recv()
     ec[3].wait_recv()
-    total = project(0, [jnp.zeros((CH, 512), F32)] * 2)
-    total = project(1, total)
+    weights_here(1)
+    weights_here(2)
+    early = [project(0, c) + project(1, c) for c in range(2)]
     weights_last(4)
     ec[6].wait_recv()
     ec[7].wait_recv()
-    total = project(2, total)
-    total = project(3, total)
-    for c in range(2):
-        out = total[c].astype(BF16)
-        for n, slot in ((N2, O2), (N1, O1), (NM, OM), (N0, O0)):
-            place = 2 * lax.rem(chunk_of[slot], 4)
-            proj[c, pl.ds(place, 2)] = out[n * 32 : (n + 1) * 32].reshape(2, 16, 512)
-    for c in ec + [c for copies in wc for c in copies]:
-        c.wait_send()
+    weights_here(3)
+    weights_here(4)
 
     mine = me // 8 == xh
 
@@ -417,17 +414,23 @@
         target = group(8 * xh + m, (t, opp)[c])
         return remote(proj.at[c, m], pieces.at[me], a_send.at[c, n], a_recv.at[me], target)
 
-    def first_copies(act):
+    def first_copies(c, act):
         for n in range(1, 8):
-            for c in range(2):
-                act(piece_copy(n, c))
-        act(piece_copy(0, 1))
-
-        @pl.when(jnp.logical_not(mine))
-        def _():
-            act(piece_copy(0, 0))
-
-    first_copies(lambda c: c.start())
+            act(piece_copy(n, c))
+        if c:
+            act(piece_copy(0, 1))
+        else:
+
+            @pl.when(jnp.logical_not(mine))
+            def _():
+                act(piece_copy(0, 0))
+
+    for c in range(2):
+        out = (early[c] + project(2, c) + project(3, c)).astype(BF16)
+        for n, slot in ((N2, O2), (N1, O1), (NM, OM), (N0, O0)):
+            place = 2 * lax.rem(chunk_of[slot], 4)
+            proj[c, pl.ds(place, 2)] = out[n * 32 : (n + 1) * 32].reshape(2, 16, 512)
+        first_copies(c, lambda copy: copy.start())
 
     @pl.when(mine)
     def _():
@@ -464,23 +467,25 @@
     for n in range(16):
         for s in range(2):
             feats[s * 256 + n * 16 : s * 256 + n * 16 + 16, :] = arrive[n, s]
-    first_copies(lambda c: c.wait_send())
-    for c in s_copies + second:
+    for c in range(2):
+        first_copies(c, lambda copy: copy.wait_send())
+    for c in s_copies + second + ec + [c for copies in wc for c in copies]:
         c.wait_send()
 
 
-def place_kernel(feats, text, counts, offsets, out):
+def place_kernel(feats, text_hbm, counts, offsets, out, text, sem):
+    copy = pltpu.make_async_copy(text_hbm, text, sem)
+    copy.start()
     me = lax.axis_index("section") * 2 + lax.axis_index("dp")
     rows = counts[me] * 256
     offset = offsets[me]
     seq = text.shape[0]
-    for r0 in range(0, seq, 256):
-        r = lax.broadcasted_iota(jnp.int32, (256, 512), 0) + r0 - offset
-        c = lax.broadcasted_iota(jnp.int32, (256, 512), 1)
-        pick = (r == c).astype(F32).astype(BF16)
-        moved = jnp.dot(pick, feats[...], preferred_element_type=F32)
-        inside = (r >= 0) & (r < rows)
-        out[r0 : r0 + 256, :] = jnp.where(inside, moved, text[r0 : r0 + 256, :].astype(F32)).astype(BF16)
+    r = lax.broadcasted_iota(jnp.int32, (seq, 512), 0) - offset
+    c = lax.broadcasted_iota(jnp.int32, (seq, 512), 1)
+    pick = (r == c).astype(F32).astype(BF16)
+    moved = jnp.dot(pick, feats[...], preferred_element_type=F32).astype(BF16)
+    copy.wait()
+    out[...] = jnp.where((r >= 0) & (r < rows), moved, text[...])
 
 
 def spec(space):
@@ -562,9 +567,10 @@
     out = pl.pallas_call(
         place_kernel,
         out_shape=jax.ShapeDtypeStruct(text_embed.shape[1:], BF16),
-        in_specs=[spec(VMEM)] * 2 + [spec(smem)] * 2,
+        in_specs=[spec(s) for s in (VMEM, pl.ANY, smem, smem)],
         out_specs=spec(VMEM),
-        compiler_params=pltpu.CompilerParams(vmem_limit_bytes=32 * 1024 * 1024),
+        scratch_shapes=[VMEM(text_embed.shape[1:], BF16), pltpu.SemaphoreType.DMA],
+        compiler_params=pltpu.CompilerParams(vmem_limit_bytes=62 * 1024 * 1024),
         name="place",
     )(feats, text_embed[0], tile_counts, image_offsets)
     return out[None]

time: 154 us -> 152 us (0.987)
    pallas_call x1, Pallas kernels: 151 us -> 149 us  [shards(): pl.pallas_call(encode_kernel, out_shape=jax.ShapeDtypeStruct((512, 512),...]
where the time goes in v4:
time: 152 us
  Pallas kernels  152 us (100%)
    pallas_call x1, Pallas kernels, shards(): pl.pallas_call(encode_kernel, out_shape=jax.ShapeDtypeStruct((512, 512),...  149 us
    pallas_call x1, Pallas kernels, shards(): pl.pallas_call(place_kernel, out_shape=jax.ShapeDtypeStruct(text_embed.sh...  3.25 us

profile of v4, /device:TPU:1, one launch (start us, length us, event | category | flops | bytes accessed | tf_op | source)
XLA Modules:
  0.0 152.2 jit_solution(3618384304225061272)
XLA Ops:
  0.0 148.8 %encode.1.feats = bf16[512,512]{1,0:T(8,128)(2,1)} custom-call(bf16[128,3200]{1,0:T(8,128)(2,1)} %bitcast.5, f32[3200]{0:T(1024)} %gain.1, bf16[3,3200,384]{2,1,0:T(8,128)(2,1)} %bitcast.4, f32[384]{0:T(512)} %q_gain.1, f32[384]{0:T(512)} %k_gain.1, f32[3200]{0:T(1024)} %layer_scale.1, bf16[384,3200]{1,0:T(8,128)(2,1)} %wo_hbm.1, bf16[12800,512]{1,0:T(8,128)(2,1)} %wp_hbm.1, ...), custom_call_target="tpu_custom_call" | custom-call | tf_op jit(solution)/shard_map/encode/pallas_call | solution.py:513
  148.8 3.3 %place.1 = bf16[768,512]{1,0:T(8,128)(2,1)} custom-call(bf16[512,512]{1,0:T(8,128)(2,1)} %encode.1.feats, bf16[768,512]{1,0:T(8,128)(2,1)} %bitcast.6, s32[16]{0:T(128)} %counts.3, s32[16]{0:T(128)} %offsets.1), custom_call_target="tpu_custom_call" | custom-call | tf_op jit(solution)/shard_map/place/pallas_call | solution.py:567

commit v5 on v4

--- a/solution.py
+++ b/solution.py
@@ -349,13 +349,13 @@
     rc[5].start()
     for i in (8, 10):
         rc[i].start()
-    weights_forward(1)
     branch(N0, 1)
     weights_cross(4)
     add(6)
     rc[9].start()
     add(7)
     rc[11].start()
+    weights_forward(1)
     weights_turn(3)
 
     def encode(row0):
@@ -392,9 +392,9 @@
         return jnp.dot(x, wp[c, ab * D : (ab + 1) * D, :], preferred_element_type=F32)
 
     forward(0)
+    forward(1)
     weights_forward(4)
     weights_last(3)
-    forward(1)
     own_copies[1].wait()
     ec[2].wait_recv()
     ec[3].wait_recv()

time: 152 us -> 152 us (level)
  no operation moved by 1% of the time
where the time goes in v5:
time: 152 us
  Pallas kernels  152 us (100%)
    pallas_call x1, Pallas kernels, shards(): pl.pallas_call(encode_kernel, out_shape=jax.ShapeDtypeStruct((512, 512),...  148 us
    pallas_call x1, Pallas kernels, shards(): pl.pallas_call(place_kernel, out_shape=jax.ShapeDtypeStruct(text_embed.sh...  3.25 us

profile of v5, /device:TPU:1, one launch (start us, length us, event | category | flops | bytes accessed | tf_op | source)
XLA Modules:
  0.0 151.9 jit_solution(10903727182025029425)
XLA Ops:
  0.0 148.5 %encode.1.feats = bf16[512,512]{1,0:T(8,128)(2,1)} custom-call(bf16[128,3200]{1,0:T(8,128)(2,1)} %bitcast.5, f32[3200]{0:T(1024)} %gain.1, bf16[3,3200,384]{2,1,0:T(8,128)(2,1)} %bitcast.4, f32[384]{0:T(512)} %q_gain.1, f32[384]{0:T(512)} %k_gain.1, f32[3200]{0:T(1024)} %layer_scale.1, bf16[384,3200]{1,0:T(8,128)(2,1)} %wo_hbm.1, bf16[12800,512]{1,0:T(8,128)(2,1)} %wp_hbm.1, ...), custom_call_target="tpu_custom_call" | custom-call | tf_op jit(solution)/shard_map/encode/pallas_call | solution.py:513
  148.5 3.3 %place.1 = bf16[768,512]{1,0:T(8,128)(2,1)} custom-call(bf16[512,512]{1,0:T(8,128)(2,1)} %encode.1.feats, bf16[768,512]{1,0:T(8,128)(2,1)} %bitcast.6, s32[16]{0:T(128)} %counts.3, s32[16]{0:T(128)} %offsets.1), custom_call_target="tpu_custom_call" | custom-call | tf_op jit(solution)/shard_map/place/pallas_call | solution.py:567

commit v6 on v5

--- a/solution.py
+++ b/solution.py
@@ -405,7 +405,6 @@
     ec[6].wait_recv()
     ec[7].wait_recv()
     weights_here(3)
-    weights_here(4)
 
     mine = me // 8 == xh
 
@@ -426,7 +425,10 @@
                 act(piece_copy(0, 0))
 
     for c in range(2):
-        out = (early[c] + project(2, c) + project(3, c)).astype(BF16)
+        out = early[c] + project(2, c)
+        if c == 0:
+            weights_here(4)
+        out = (out + project(3, c)).astype(BF16)
         for n, slot in ((N2, O2), (N1, O1), (NM, OM), (N0, O0)):
             place = 2 * lax.rem(chunk_of[slot], 4)
             proj[c, pl.ds(place, 2)] = out[n * 32 : (n + 1) * 32].reshape(2, 16, 512)

time: 152 us -> 152 us (level)
  no operation moved by 1% of the time
where the time goes in v6:
time: 152 us
  Pallas kernels  152 us (100%)
    pallas_call x1, Pallas kernels, shards(): pl.pallas_call(encode_kernel, out_shape=jax.ShapeDtypeStruct((512, 512),...  148 us
    pallas_call x1, Pallas kernels, shards(): pl.pallas_call(place_kernel, out_shape=jax.ShapeDtypeStruct(text_embed.sh...  3.25 us

profile of v6, /device:TPU:1, one launch (start us, length us, event | category | flops | bytes accessed | tf_op | source)
XLA Modules:
  0.0 151.7 jit_solution(12122568808737630103)
XLA Ops:
  0.0 148.3 %encode.1.feats = bf16[512,512]{1,0:T(8,128)(2,1)} custom-call(bf16[128,3200]{1,0:T(8,128)(2,1)} %bitcast.5, f32[3200]{0:T(1024)} %gain.1, bf16[3,3200,384]{2,1,0:T(8,128)(2,1)} %bitcast.4, f32[384]{0:T(512)} %q_gain.1, f32[384]{0:T(512)} %k_gain.1, f32[3200]{0:T(1024)} %layer_scale.1, bf16[384,3200]{1,0:T(8,128)(2,1)} %wo_hbm.1, bf16[12800,512]{1,0:T(8,128)(2,1)} %wp_hbm.1, ...), custom_call_target="tpu_custom_call" | custom-call | tf_op jit(solution)/shard_map/encode/pallas_call | solution.py:515
  148.3 3.3 %place.1 = bf16[768,512]{1,0:T(8,128)(2,1)} custom-call(bf16[512,512]{1,0:T(8,128)(2,1)} %encode.1.feats, bf16[768,512]{1,0:T(8,128)(2,1)} %bitcast.6, s32[16]{0:T(128)} %counts.3, s32[16]{0:T(128)} %offsets.1), custom_call_target="tpu_custom_call" | custom-call | tf_op jit(solution)/shard_map/place/pallas_call | solution.py:569
